TPU v7x, 512 devices: a whole 4x8x8 slice. The times are simulated.
512 devices in a mesh: dp: 64 (over z, x, core), ctx: 8 (over y).
Axes of the slice: x: 4, y: 8, z: 8, core: 2. Of those that a mesh axis runs over, the one named last changes fastest.
Arguments:
- q_short: bfloat16 [65536, 2048], P(('dp', 'ctx')), may hold values from -32 to 32
- k_short: bfloat16 [65536, 512], P(('dp', 'ctx')), may hold values from -32 to 32
- v_short: bfloat16 [65536, 512], P(('dp', 'ctx')), may hold values from -6 to 6
- short_lengths: int32 [64, 8, 2, 3], P(None, 'ctx'), may hold values from 1 to 48, 64 in all within a row
- bin_dest: int32 [64, 8, 2], P(None, 'ctx'), may hold values from 0 to 63, as said below
- q_long: bfloat16 [65536, 2048], P(('dp', 'ctx')), may hold values from -32 to 32
- k_long: bfloat16 [65536, 512], P(('dp', 'ctx')), may hold values from -32 to 32
- v_long: bfloat16 [65536, 512], P(('dp', 'ctx')), may hold values from -6 to 6
- long_lengths: int32 [64, 3], P('dp'), may hold values from 1 to 960, 1024 in all within a row
Outputs:
- out_short: bfloat16 [65536, 2048], P(('dp', 'ctx'))
- out_long: bfloat16 [65536, 2048], P(('dp', 'ctx'))
Inputs may be any that keep to these rules, and one draw needn't show every extreme that they name: bin_dest[s, c, j] = s XOR m[c, j], where for each c the 2 masks m[c, j] are distinct; so every dp rank receives exactly 2 bins at each ctx index, one of each j. At ctx index 0 one of the masks is 63. `short_lengths`: each bin holds 3 documents that fill its 64 tokens. `long_lengths`: the 3 documents of a region fill its 1024 tokens.
All inputs are finite; a program needn't handle non-finite values.
Results may differ from a plain program's by a relative error of at most 0.009.
Values may be sent and summed in bfloat16 or wider, within the bound.
A program may use at most 64 MiB of HBM per device.

v0:
```python
import math

import jax
import jax.numpy as jnp
from jax import lax
from jax.sharding import PartitionSpec as P

QHEADS = 16
KVHEADS = 4
HEAD_DIM = 128
BIN_LEN = 64
DOCS_BIN = 3


THETA = 500000.0
NEGATIVE = -1e30


def from_partner(shard, axis, distance):
    return lax.ppermute(shard, axis, [(i, i ^ 1 << distance) for i in range(lax.axis_size(axis))])


def doc_layout(lengths, extent):
    doc_ends = jnp.cumsum(lengths, axis=-1)
    doc_starts = doc_ends - lengths
    token_index = jnp.arange(extent, dtype=jnp.int32)
    covered = (token_index[:, None] >= doc_starts[..., None, :]) & (
        token_index[:, None] < doc_ends[..., None, :]
    )
    doc_labels = jnp.arange(lengths.shape[-1], dtype=jnp.int32)
    segment = jnp.sum(jnp.where(covered, doc_labels, 0), axis=-1)
    offset = jnp.sum(
        jnp.where(covered, token_index[:, None] - doc_starts[..., None, :], 0), axis=-1
    )
    return (segment, offset)


def rotary(values, position, heads):
    row_count = values.shape[0]
    half_dim = HEAD_DIM // 2
    inverse = THETA ** (-(jnp.arange(half_dim, dtype=jnp.float32) * (2.0 / HEAD_DIM)))
    angles = position.astype(jnp.float32)[:, None] * inverse[None, :]
    cosine = jnp.cos(angles)[:, None, :]
    sine_part = jnp.sin(angles)[:, None, :]
    shaped = values.astype(jnp.float32).reshape(row_count, heads, HEAD_DIM)
    first_half = shaped[..., :half_dim]
    second_half = shaped[..., half_dim:]
    turned = jnp.concatenate(
        [
            first_half * cosine - second_half * sine_part,
            second_half * cosine + first_half * sine_part,
        ],
        axis=-1,
    )
    return turned.reshape(row_count, heads * HEAD_DIM).astype(jnp.bfloat16)


def tile_attention(query_rows, key_rows, value_rows, segment):
    row_count = query_rows.shape[0]
    tile_rows = 128
    tile_count = row_count // tile_rows
    group_size = QHEADS // KVHEADS
    query_tiles = query_rows.reshape(tile_count, tile_rows, KVHEADS, group_size, HEAD_DIM)
    key_tiles = key_rows.reshape(tile_count, tile_rows, KVHEADS, HEAD_DIM)
    value_tiles = value_rows.reshape(tile_count, tile_rows, KVHEADS, HEAD_DIM)
    segment_tiles = segment.reshape(tile_count, tile_rows)
    tile_order = jnp.arange(tile_rows, dtype=jnp.int32)
    allowed = (segment_tiles[:, :, None] == segment_tiles[:, None, :]) & (
        tile_order[None, None, :] <= tile_order[None, :, None]
    )
    mask_wide = allowed[:, None, None]
    scores = jnp.einsum(
        "brkgd,bckd->bkgrc", query_tiles, key_tiles, preferred_element_type=jnp.float32
    ) * (1.0 / math.sqrt(HEAD_DIM))
    scores = jnp.where(mask_wide, scores, NEGATIVE)
    row_max = jnp.max(scores, axis=-1, keepdims=True)
    weight = jnp.where(mask_wide, jnp.exp(scores - row_max), 0.0)
    weight_sum = jnp.sum(weight, axis=-1)
    blended = jnp.einsum(
        "bkgrc,bckd->brkgd",
        weight.astype(jnp.bfloat16),
        value_tiles,
        preferred_element_type=jnp.float32,
    )
    blended = blended / jnp.transpose(weight_sum, (0, 3, 1, 2))[..., None]
    return blended.reshape(row_count, QHEADS * HEAD_DIM).astype(jnp.bfloat16)


def labelled(segment):
    bin_ids = jnp.arange(segment.shape[0], dtype=jnp.int32)[:, None]
    return (segment + bin_ids * DOCS_BIN).reshape(-1)


def local(q_short, k_short, v_short, short_lengths, bin_dest, q_long, k_long, v_long, long_lengths):
    dp_count = lax.axis_size("dp")
    ctx_count = lax.axis_size("ctx")
    dp_index = lax.axis_index("dp")
    ctx_index = lax.axis_index("ctx")
    group_size = QHEADS // KVHEADS
    score_scale = 1.0 / math.sqrt(HEAD_DIM)
    query_width = QHEADS * HEAD_DIM
    key_width = KVHEADS * HEAD_DIM
    span_rows = q_long.shape[0]
    region = span_rows * ctx_count
    region_segment, region_position = doc_layout(long_lengths[0], region)
    first_row = ctx_index * span_rows
    my_segment = lax.dynamic_slice_in_dim(region_segment, first_row, span_rows, 0)
    my_position = lax.dynamic_slice_in_dim(region_position, first_row, span_rows, 0)
    query_long = rotary(q_long, my_position, QHEADS)
    key_long = rotary(k_long, my_position, KVHEADS)
    query_groups = query_long.reshape(span_rows, KVHEADS, group_size, HEAD_DIM)
    my_rows = first_row + jnp.arange(span_rows, dtype=jnp.int32)
    run_max = jnp.full((KVHEADS, group_size, span_rows), NEGATIVE, jnp.float32)
    piece_keys = lax.all_gather(key_long, "ctx", axis=0, tiled=True)
    piece_values = lax.all_gather(v_long, "ctx", axis=0, tiled=True)
    piece_rows = piece_keys.shape[0]
    key_index = jnp.arange(piece_rows, dtype=jnp.int32)
    allowed = (my_segment[:, None] == region_segment[None, :]) & (
        key_index[None, :] <= my_rows[:, None]
    )
    scores = (
        jnp.einsum(
            "rkgd,ckd->kgrc",
            query_groups,
            piece_keys.reshape(piece_rows, KVHEADS, HEAD_DIM),
            preferred_element_type=jnp.float32,
        )
        * score_scale
    )
    scores = jnp.where(allowed, scores, NEGATIVE)
    new_max = jnp.maximum(run_max, jnp.max(scores, axis=-1))
    weight = jnp.where(allowed, jnp.exp(scores - new_max[..., None]), 0.0)
    new_total = jnp.sum(weight, axis=-1)
    new_acc = jnp.einsum(
        "kgrc,ckd->kgrd",
        weight.astype(jnp.bfloat16),
        piece_values.reshape(piece_rows, KVHEADS, HEAD_DIM),
        preferred_element_type=jnp.float32,
    )
    finished = new_acc / new_total[..., None]
    out_long = (
        jnp.transpose(finished, (2, 0, 1, 3)).reshape(span_rows, query_width).astype(jnp.bfloat16)
    )
    bin_count = short_lengths.shape[2]
    section_count = dp_count.bit_length() - 1
    home_lengths = lax.dynamic_index_in_dim(short_lengths[:, 0], dp_index, 0, keepdims=False)
    home_dest = lax.dynamic_index_in_dim(bin_dest[:, 0], dp_index, 0, keepdims=False)
    home_segment, home_position = doc_layout(home_lengths, BIN_LEN)
    flat_position = home_position.reshape(-1)
    query_home = rotary(q_short, flat_position, QHEADS)
    key_home = rotary(k_short, flat_position, KVHEADS)
    section_bits = list(range(section_count))
    sender_order = jnp.argsort(home_dest)
    joined = jnp.concatenate([query_home, key_home, v_short], axis=1)
    row_width = joined.shape[1]
    moving = joined.reshape(bin_count, BIN_LEN, row_width)
    for bit in section_bits:
        flips = home_dest // 2**bit % 2 != dp_index // 2**bit % 2
        partner = from_partner(moving, "dp", bit)
        moving = jnp.where(flips[:, None, None], partner, moving)
    arrived = moving.reshape(bin_count * BIN_LEN, row_width)
    arrived_query = arrived[:, :query_width]
    arrived_key = arrived[:, query_width : query_width + key_width]
    arrived_value = arrived[:, query_width + key_width :]
    arrived_lengths = short_lengths[:, 0][home_dest, jnp.arange(bin_count, dtype=jnp.int32)]
    arrived_segment, unused_position = doc_layout(arrived_lengths, BIN_LEN)
    values = tile_attention(arrived_query, arrived_key, arrived_value, labelled(arrived_segment))
    row_width = values.shape[1]
    slots = values.reshape(bin_count, BIN_LEN * row_width)
    out_short = jnp.take(slots, sender_order, axis=0).reshape(bin_count * BIN_LEN, row_width)
    return (out_short, out_long)


def solution(mesh):
    in_specs = (
        P(("dp", "ctx"), None),
        P(("dp", "ctx"), None),
        P(("dp", "ctx"), None),
        P(None, "ctx", None, None),
        P(None, "ctx", None),
        P(("dp", "ctx"), None),
        P(("dp", "ctx"), None),
        P(("dp", "ctx"), None),
        P("dp", None),
    )
    out_specs = (P(("dp", "ctx"), None), P(("dp", "ctx"), None))
    return jax.shard_map(local, mesh=mesh, in_specs=in_specs, out_specs=out_specs, check_vma=False)
```

profile of v0, /device:TPU:1, one launch (start us, length us, event | category | flops | bytes accessed | tf_op | source)
XLA Modules:
  0.0 187.7 jit_solution(2117379052073205452)
XLA Ops:
  7.3 0.8 constant_dynamic-slice_fusion
  8.8 0.8 reduce-window.4
  9.6 0.7 fusion.39
  10.2 1.0 copy.100
  11.4 0.3 multiply_cosine_fusion
  11.8 0.7 pad_maximum_fusion.5
  12.7 1.1 convert_bitcast_fusion.1
  14.1 0.5 subtract_convert_fusion.1
  14.6 0.3 pad_maximum_fusion.1
  15.2 0.3 subtract_convert_fusion.2
  15.8 8.8 %collective-permute-start = (bf16[2,64,3072]{2,1,0:T(8,128)(2,1)S(1)}, bf16[2,64,3072]{2,1,0:T(8,128)(2,1)S(1)}, u32[]{:S(2)}, u32[]{:S(2)}) collective-permute-start(bf16[2,64,3072]{2,1,0:T(8,128)(2,1)S(1)} %bitcast.107), channel_id=1, source_target_pairs={{0,8},{8,0},{16,24},{24,16},{32,40},{40,32},{48,56},{56,48},{64,72... | collective-permute-start | bytes 2359304 | tf_op jit(solution)/shard_map/ppermute | solution.py:20
  25.1 0.6 gather_fusion
  26.3 0.2 collective-permute-done
  26.5 1.0 broadcast_select_fusion
  27.5 1.9 %collective-permute-start.1 = (bf16[2,64,3072]{2,1,0:T(8,128)(2,1)}, bf16[2,64,3072]{2,1,0:T(8,128)(2,1)}, u32[]{:S(2)}, u32[]{:S(2)}) collective-permute-start(bf16[2,64,3072]{2,1,0:T(8,128)(2,1)} %broadcast_select_fusion), channel_id=1, source_target_pairs={{0,16},{8,24},{16,0},{24,8},{32,48},{40,56},{48,32},{56,40},{64,80... | collective-permute-start | bytes 2359304 | tf_op jit(solution)/shard_map/ppermute | solution.py:20
  29.7 0.6 sort.17
  30.3 0.3 fusion.45
  30.7 17.8 %collective-permute-done.1 = bf16[2,64,3072]{2,1,0:T(8,128)(2,1)} collective-permute-done((bf16[2,64,3072]{2,1,0:T(8,128)(2,1)}, bf16[2,64,3072]{2,1,0:T(8,128)(2,1)}, u32[]{:S(2)}, u32[]{:S(2)}) %collective-permute-start.1) | collective-permute-done | bytes 786464 | tf_op jit(solution)/shard_map/ppermute | solution.py:20
  48.5 2.4 %broadcast_select_fusion.1 = bf16[2,64,3072]{2,1,0:T(8,128)(2,1)} fusion(bf16[2,64,3072]{2,1,0:T(8,128)(2,1)} %collective-permute-done.1, bf16[2,64,3072]{2,1,0:T(8,128)(2,1)} %broadcast_select_fusion, pred[2]{0:T(512)(128)(4,1)S(1)} %get-tuple-element.38), kind=kLoop, calls=%fused_computation.28 | loop fusion | flops 393216 | bytes 2359298 | tf_op jit(solution)/shard_map/jit(_where)/select_n | solution.py:160
  50.9 1.9 %collective-permute-start.2 = (bf16[2,64,3072]{2,1,0:T(8,128)(2,1)}, bf16[2,64,3072]{2,1,0:T(8,128)(2,1)S(1)}, u32[]{:S(2)}, u32[]{:S(2)}) collective-permute-start(bf16[2,64,3072]{2,1,0:T(8,128)(2,1)} %broadcast_select_fusion.1), channel_id=1, source_target_pairs={{0,32},{8,40},{16,48},{24,56},{32,0},{40,8},{48,16},{56,24},{64,96... | collective-permute-start | bytes 2359304 | tf_op jit(solution)/shard_map/ppermute | solution.py:20
  53.4 0.7 subtract_convert_fusion
  54.0 0.3 pad_maximum_fusion.3
  54.4 17.9 %collective-permute-done.2 = bf16[2,64,3072]{2,1,0:T(8,128)(2,1)S(1)} collective-permute-done((bf16[2,64,3072]{2,1,0:T(8,128)(2,1)}, bf16[2,64,3072]{2,1,0:T(8,128)(2,1)S(1)}, u32[]{:S(2)}, u32[]{:S(2)}) %collective-permute-start.2) | collective-permute-done | bytes 786464 | tf_op jit(solution)/shard_map/ppermute | solution.py:20
  72.3 1.3 broadcast_select_fusion.2
  73.7 1.9 %collective-permute-start.3 = (bf16[2,64,3072]{2,1,0:T(8,128)(2,1)S(1)}, bf16[2,64,3072]{2,1,0:T(8,128)(2,1)S(1)}, u32[]{:S(2)}, u32[]{:S(2)}) collective-permute-start(bf16[2,64,3072]{2,1,0:T(8,128)(2,1)S(1)} %broadcast_select_fusion.2), channel_id=1, source_target_pairs={{0,64},{8,72},{16,80},{24,88},{32,96},{40,104},{48,112},{56,120},{... | collective-permute-start | bytes 2359304 | tf_op jit(solution)/shard_map/ppermute | solution.py:20
  75.8 5.9 %fusion = (f32[4,4,128]{2,1,0:T(4,128)S(1)}, f32[4,1024,128,4]{2,1,3,0:T(8,128)}) fusion(pred[128,1024]{0,1:T(8,128)(4,1)S(1)} %fusion.19, bf16[1024,4,128,1]{0,2,3,1:T(8,128)(2,1)} %bitcast.111, bf16[128,4,4,128]{3,0,2,1:T(8,128)(2,1)S(1)} %bitcast.106), kind=kOutput, calls=%fused_computation.5 | convolution fusion | flops 543160320 | bytes 10100736 | tf_op jit(solution)/shard_map/rkgd,ckd->kgrc/dot_general | solution.py:122
  81.8 10.7 %collective-permute-done.3 = bf16[2,64,3072]{2,1,0:T(8,128)(2,1)S(1)} collective-permute-done((bf16[2,64,3072]{2,1,0:T(8,128)(2,1)S(1)}, bf16[2,64,3072]{2,1,0:T(8,128)(2,1)S(1)}, u32[]{:S(2)}, u32[]{:S(2)}) %collective-permute-start.3) | collective-permute-done | bytes 786464 | tf_op jit(solution)/shard_map/ppermute | solution.py:20
  92.6 1.9 %collective-permute-start.4 = (bf16[2,64,3072]{2,1,0:T(8,128)(2,1)S(1)}, bf16[2,64,3072]{2,1,0:T(8,128)(2,1)}, u32[]{:S(2)}, u32[]{:S(2)}) collective-permute-start(bf16[2,64,3072]{2,1,0:T(8,128)(2,1)S(1)} %broadcast_select_fusion.3), channel_id=1, source_target_pairs={{0,128},{8,136},{16,144},{24,152},{32,160},{40,168},{48,176},{56,1... | collective-permute-start | bytes 2359304 | tf_op jit(solution)/shard_map/ppermute | solution.py:20
  94.6 4.1 %all-gather.5.cloned.1.call-done = bf16[1024,512]{1,0:T(8,128)(2,1)} async-done(((bf16[128,512]{1,0:T(8,128)(2,1)}), bf16[1024,512]{1,0:T(8,128)(2,1)}) %all-gather.5.cloned.1.call-update) | async-done | bytes 1048592 | tf_op jit(solution)/shard_map/all_gather | solution.py:115
  98.7 1.5 copy.86
  100.2 4.6 %fusion.1 = f32[4,4,128]{2,1,0:T(4,128)S(1)} fusion(f32[4,1024,128,4]{2,1,3,0:T(8,128)} %get-tuple-element.43, f32[4,4,128]{2,1,0:T(4,128)S(1)} %broadcast_maximum_fusion, pred[128,1024]{0,1:T(8,128)(4,1)S(1)} %fusion.19), kind=kLoop, calls=%fused_computation.6 | loop fusion | flops 10483712 | bytes 8536064 | tf_op jit(solution)/shard_map/reduce_sum | solution.py:133
  104.8 26.9 %collective-permute-done.4 = bf16[2,64,3072]{2,1,0:T(8,128)(2,1)} collective-permute-done((bf16[2,64,3072]{2,1,0:T(8,128)(2,1)S(1)}, bf16[2,64,3072]{2,1,0:T(8,128)(2,1)}, u32[]{:S(2)}, u32[]{:S(2)}) %collective-permute-start.4) | collective-permute-done | bytes 786464 | tf_op jit(solution)/shard_map/ppermute | solution.py:20
  131.7 1.3 broadcast_select_fusion.4
  133.0 4.7 %collective-permute-start.5 = (bf16[2,64,3072]{2,1,0:T(8,128)(2,1)S(1)}, bf16[2,64,3072]{2,1,0:T(8,128)(2,1)S(1)}, u32[]{:S(2)}, u32[]{:S(2)}) collective-permute-start(bf16[2,64,3072]{2,1,0:T(8,128)(2,1)S(1)} %broadcast_select_fusion.4), channel_id=1, source_target_pairs={{0,256},{8,264},{16,272},{24,280},{32,288},{40,296},{48,304},{56,3... | collective-permute-start | bytes 2359304 | tf_op jit(solution)/shard_map/ppermute | solution.py:20
  137.7 2.2 %divide_convert_fusion = bf16[128,4,4,128]{0,3,2,1:T(8,128)(2,1)S(1)} fusion(bf16[1024,4,128,1]{0,2,3,1:T(8,128)(2,1)S(1)} %bitcast.116, f32[4,1024,128,4]{2,1,3,0:T(8,128)S(1)} %copy-done.1, f32[4,4,128]{2,1,0:T(4,128)S(1)} %broadcast_maximum_fusion, pred[128,1024]{0,1:T(8,128)(4,1)S(1)} %fusion.19, f32[128,4,4]{0,2,1:T(4,128)S(1)} %bitcast.126), kind=kOutput, calls=%fused_computation.17 | convolution fusion | flops 547880960 | bytes 10108928 | tf_op jit(solution)/shard_map/kgrc,ckd->kgrd/dot_general | solution.py:134
  139.9 1.0 copy.88
  140.9 33.6 %collective-permute-done.5 = bf16[2,64,3072]{2,1,0:T(8,128)(2,1)S(1)} collective-permute-done((bf16[2,64,3072]{2,1,0:T(8,128)(2,1)S(1)}, bf16[2,64,3072]{2,1,0:T(8,128)(2,1)S(1)}, u32[]{:S(2)}, u32[]{:S(2)}) %collective-permute-start.5) | collective-permute-done | bytes 786464 | tf_op jit(solution)/shard_map/ppermute | solution.py:20
  174.8 0.3 copy.74
  175.3 0.4 fusion.48
  175.7 0.2 fusion.13
  175.9 0.3 divide_convert_fusion.1
  176.2 0.4 copy.78
  176.8 0.4 fusion.47
  177.2 0.9 gather_fusion.1
  178.1 0.9 gather_fusion.2
  179.0 0.5 pad_maximum_fusion.2
  179.4 0.5 gather.11
  179.9 0.9 broadcast_select_fusion.6
  (71 shorter events, 4.6 us)
Async XLA Ops:
  7.2 17.7 %copy-start = (s32[64,1,2]{0,2,1:T(2,128)S(1)}, s32[64,1,2]{0,2,1:T(2,128)}, u32[]{:S(2)}) copy-start(s32[64,1,2]{0,2,1:T(2,128)} %param.13) | copy-start | bytes 1540
  7.2 17.6 %copy-start.5 = (s32[64,1,2,3]{0,2,3,1:T(2,128)S(1)}, s32[64,1,2,3]{0,2,3,1:T(2,128)}, u32[]{:S(2)}) copy-start(s32[64,1,2,3]{0,2,3,1:T(2,128)} %param.12) | copy-start | bytes 4612
  7.2 7.9 %copy-start.3 = (bf16[128,512]{1,0:T(8,128)(2,1)S(1)}, bf16[128,512]{1,0:T(8,128)(2,1)}, u32[]{:S(2)}) copy-start(bf16[128,512]{1,0:T(8,128)(2,1)} %param.10) | copy-start | bytes 393220
  7.2 8.5 %copy-start.4 = (bf16[128,512]{1,0:T(8,128)(2,1)S(1)}, bf16[128,512]{1,0:T(8,128)(2,1)}, u32[]{:S(2)}) copy-start(bf16[128,512]{1,0:T(8,128)(2,1)} %param.11) | copy-start | bytes 393220
  7.2 19.0 %copy-start.2 = (bf16[128,2048]{1,0:T(8,128)(2,1)S(1)}, bf16[128,2048]{1,0:T(8,128)(2,1)}, u32[]{:S(2)}) copy-start(bf16[128,2048]{1,0:T(8,128)(2,1)} %param.14) | copy-start | bytes 1572868
  7.2 68.6 %all-gather.3.cloned.1.call-start = ((), (), s32[]{:S(2)}) async-start(), calls=%async_computation | async-start | bytes 1179648 | tf_op jit(solution)/shard_map/all_gather | solution.py:114
  12.5 86.2 %all-gather.5.cloned.1.call-start = ((), (), s32[]{:S(2)}) async-start(), calls=%async_computation.1 | async-start | bytes 1179648 | tf_op jit(solution)/shard_map/all_gather | solution.py:115
  15.8 10.7 %collective-permute-start = (bf16[2,64,3072]{2,1,0:T(8,128)(2,1)S(1)}, bf16[2,64,3072]{2,1,0:T(8,128)(2,1)S(1)}, u32[]{:S(2)}, u32[]{:S(2)}) collective-permute-start(bf16[2,64,3072]{2,1,0:T(8,128)(2,1)S(1)} %bitcast.107), channel_id=1, source_target_pairs={{0,8},{8,0},{16,24},{24,16},{32,40},{40,32},{48,56},{56,48},{64,72... | collective-permute-start | bytes 2359304 | tf_op jit(solution)/shard_map/ppermute | solution.py:20
  27.5 21.0 %collective-permute-start.1 = (bf16[2,64,3072]{2,1,0:T(8,128)(2,1)}, bf16[2,64,3072]{2,1,0:T(8,128)(2,1)}, u32[]{:S(2)}, u32[]{:S(2)}) collective-permute-start(bf16[2,64,3072]{2,1,0:T(8,128)(2,1)} %broadcast_select_fusion), channel_id=1, source_target_pairs={{0,16},{8,24},{16,0},{24,8},{32,48},{40,56},{48,32},{56,40},{64,80... | collective-permute-start | bytes 2359304 | tf_op jit(solution)/shard_map/ppermute | solution.py:20
  50.9 21.4 %collective-permute-start.2 = (bf16[2,64,3072]{2,1,0:T(8,128)(2,1)}, bf16[2,64,3072]{2,1,0:T(8,128)(2,1)S(1)}, u32[]{:S(2)}, u32[]{:S(2)}) collective-permute-start(bf16[2,64,3072]{2,1,0:T(8,128)(2,1)} %broadcast_select_fusion.1), channel_id=1, source_target_pairs={{0,32},{8,40},{16,48},{24,56},{32,0},{40,8},{48,16},{56,24},{64,96... | collective-permute-start | bytes 2359304 | tf_op jit(solution)/shard_map/ppermute | solution.py:20
  73.7 18.8 %collective-permute-start.3 = (bf16[2,64,3072]{2,1,0:T(8,128)(2,1)S(1)}, bf16[2,64,3072]{2,1,0:T(8,128)(2,1)S(1)}, u32[]{:S(2)}, u32[]{:S(2)}) collective-permute-start(bf16[2,64,3072]{2,1,0:T(8,128)(2,1)S(1)} %broadcast_select_fusion.2), channel_id=1, source_target_pairs={{0,64},{8,72},{16,80},{24,88},{32,96},{40,104},{48,112},{56,120},{... | collective-permute-start | bytes 2359304 | tf_op jit(solution)/shard_map/ppermute | solution.py:20
  92.6 39.1 %collective-permute-start.4 = (bf16[2,64,3072]{2,1,0:T(8,128)(2,1)S(1)}, bf16[2,64,3072]{2,1,0:T(8,128)(2,1)}, u32[]{:S(2)}, u32[]{:S(2)}) collective-permute-start(bf16[2,64,3072]{2,1,0:T(8,128)(2,1)S(1)} %broadcast_select_fusion.3), channel_id=1, source_target_pairs={{0,128},{8,136},{16,144},{24,152},{32,160},{40,168},{48,176},{56,1... | collective-permute-start | bytes 2359304 | tf_op jit(solution)/shard_map/ppermute | solution.py:20
  100.1 37.6 %copy-start.1 = (f32[4,1024,128,4]{2,1,3,0:T(8,128)S(1)}, f32[4,1024,128,4]{2,1,3,0:T(8,128)}, u32[]{:S(2)}) copy-start(f32[4,1024,128,4]{2,1,3,0:T(8,128)} %get-tuple-element.43) | copy-start | bytes 25165828
  133.0 41.5 %collective-permute-start.5 = (bf16[2,64,3072]{2,1,0:T(8,128)(2,1)S(1)}, bf16[2,64,3072]{2,1,0:T(8,128)(2,1)S(1)}, u32[]{:S(2)}, u32[]{:S(2)}) collective-permute-start(bf16[2,64,3072]{2,1,0:T(8,128)(2,1)S(1)} %broadcast_select_fusion.4), channel_id=1, source_target_pairs={{0,256},{8,264},{16,272},{24,280},{32,288},{40,296},{48,304},{56,3... | collective-permute-start | bytes 2359304 | tf_op jit(solution)/shard_map/ppermute | solution.py:20
Sparse Core Ops, SparseCore 0:
  12.6 43.5 all-gather.2
  58.3 40.2 all-gather.4
where the time goes:
time: 188 us
  waiting for transfers between devices  111 us (59%)
  starting transfers between devices  21.2 us (11%)
  other arithmetic  20.5 us (11%)
  between operations  14.7 us (8%)
  local copies, waits for them, and re-layouts  11.2 us (6%)
  matrix products  8.79 us (5%)
    ppermute x6, waiting for transfers between devices, from_partner(): lax.ppermute(shard, axis, [(i, i ^ 1 << distance) for i in range(lax.axis...  107 us
    ppermute x6, starting transfers between devices, from_partner(): lax.ppermute(shard, axis, [(i, i ^ 1 << distance) for i in range(lax.axis...  21.1 us
    select_n x6, other arithmetic, local(): moving = jnp.where(flips[:, None, None], partner, moving)  6.4 us
    dot_general x1, matrix products, local(): jnp.einsum('rkgd,ckd->kgrc', query_groups, piece_keys.reshape(piece_rows,...  5.92 us
    reduce_sum x1, other arithmetic, local(): new_total = jnp.sum(weight, axis=-1)  4.64 us
    all_gather x1, waiting for transfers between devices, local(): piece_values = lax.all_gather(v_long, 'ctx', axis=0, tiled=True)  4.1 us
  transfers between devices with their start and end apart: 8, of which 7 were waited for; matrix products, arithmetic and copies ran while one was open for 15% of the time, Pallas kernels for 0%

commit v1 on v0

v1 whole, which is shorter than its diff:
```python
import functools
import math

import jax
import jax.numpy as jnp
import numpy as np
from jax import lax
from jax.experimental import pallas as pl
from jax.experimental.pallas import tpu as pltpu
from jax.sharding import PartitionSpec as P

QHEADS = 16
KVHEADS = 4
GROUP = QHEADS // KVHEADS
HEAD_DIM = 128
HALF = HEAD_DIM // 2
WIDE = GROUP * HEAD_DIM
BIN_LEN = 64
BINS = 2
THETA = 500000.0
NEGATIVE = -1e30
SCALE = math.log2(math.e) / math.sqrt(HEAD_DIM)

NZ, NX, NY = 8, 4, 8
CHUNKS = KVHEADS
STEPS = 8
DIRS = 4
OWN = 2 * CHUNKS
POOL = OWN + DIRS * STEPS
ROUTE = DIRS * STEPS + CHUNKS
HOPS = NY // 2
Y_SENDS = 3 * KVHEADS + KVHEADS // 2
MESH = pl.DeviceIdType.MESH


def moved(place, direction):
    z, x = divmod(place, NX)
    if direction < 2:
        x = (x + (1, -1)[direction]) % NX
    else:
        z = (z + (1, -1)[direction - 2]) % NZ
    return z * NX + x


@functools.cache
def route_table():
    table = np.zeros((NZ * NX, NZ * NX, ROUTE), np.int32)
    for mask in range(NZ * NX):
        packets = []
        for place in range(NZ * NX):
            z, x = divmod(place, NX)
            goal_z, goal_x = divmod(place ^ mask, NX)
            for chunk in range(CHUNKS):
                dz, dx = (goal_z - z) % NZ, (goal_x - x) % NX
                if dz > NZ // 2 or (dz == NZ // 2 and chunk % 2):
                    dz -= NZ
                if dx > NX // 2 or (dx == NX // 2 and (chunk // (2 if mask // NX == NZ // 2 else 1)) % 2):
                    dx -= NX
                packets.append([place, dz, dx, chunk, chunk])
        step = 0
        while any(p[1] or p[2] for p in packets):
            order = sorted(packets, key=lambda p: (-abs(p[1]) - abs(p[2]), -abs(p[1]), p[4]))
            taken, moves = set(), []
            for p in order:
                options = []
                if p[1]:
                    options.append(2 if p[1] > 0 else 3)
                if p[2]:
                    options.append(0 if p[2] > 0 else 1)
                for d in options:
                    if (p[0], d) not in taken:
                        taken.add((p[0], d))
                        moves.append((p, d))
                        break
            for p, d in moves:
                table[mask, p[0], step * DIRS + d] = p[3]
                p[0] = moved(p[0], d)
                p[2 if d < 2 else 1] -= (1, -1)[d % 2]
                p[3] = OWN + DIRS * step + d
            step += 1
        assert step <= STEPS
        for p in packets:
            table[mask, p[0], DIRS * STEPS + p[4]] = p[3]
    return table


def doc_start(lengths, index):
    first = lengths[..., 0:1]
    second = first + lengths[..., 1:2]
    return jnp.where(index >= second, second, jnp.where(index >= first, first, 0))


def turn_tables(position):
    inverse = THETA ** (-(jnp.arange(HALF, dtype=jnp.float32) * (2.0 / HEAD_DIM)))
    angles = position.astype(jnp.float32)[:, None] * inverse[None, :]
    cosine, sine = jnp.cos(angles), jnp.sin(angles)
    return jnp.concatenate([cosine, cosine], 1), jnp.concatenate([-sine, sine], 1)


def rotated(block, cosine, sine):
    wide = block.astype(jnp.float32)
    return (wide * cosine + pltpu.roll(wide, HALF, 1) * sine).astype(jnp.bfloat16)


def columns(g, width):
    return pl.ds(pl.multiple_of(g * width, width), width)


def turned_heads(q_ref, rows, g, cosine, sine):
    block = q_ref[rows, columns(g, WIDE)]
    parts = [block[:, i * HEAD_DIM : (i + 1) * HEAD_DIM] for i in range(GROUP)]
    return jnp.concatenate([rotated(part, cosine, sine) for part in parts], 0)


def side_by_side(block):
    rows = block.shape[0] // GROUP
    return jnp.concatenate([block[i * rows : (i + 1) * rows] for i in range(GROUP)], 1)


def score(query, key):
    return SCALE * lax.dot_general(
        query, key, (((1,), (1,)), ((), ())), preferred_element_type=jnp.float32
    )


def kernel(
    route_ref, order_ref, q_short, k_short, v_short, short_cos, short_sin, short_start,
    q_long, k_long, v_long, long_cos, long_sin, long_start,
    out_short, out_long,
    pool0, pool1, stage, landing, kv, query, top, total, acc, bias_ref,
    mate_send, mate_recv, route_send, route_recv, y_send, y_recv,
):
    dp, ctx = lax.axis_index("dp"), lax.axis_index("ctx")
    core, x, z = dp % 2, (dp // 2) % NX, dp // (2 * NX)
    span = q_long.shape[0]

    def at(z_to, x_to):
        return (((z_to + NZ) % NZ * NX + (x_to + NX) % NX) * 2 + core, ctx)

    mate = (dp + 1 - 2 * core, ctx)
    routes = [at(z, x + 1), at(z, x - 1), at(z + 1, x), at(z - 1, x)]
    rings = [(dp, (ctx + 1) % NY), (dp, (ctx + NY - 1) % NY)]

    barrier = pltpu.get_barrier_semaphore()
    for other in [mate, *routes, *rings]:
        pl.semaphore_signal(barrier, inc=1, device_id=other, device_id_type=MESH)
    pl.semaphore_wait(barrier, 3 + DIRS)

    def copy(source, target, send, recv, other):
        return pltpu.make_async_remote_copy(
            src_ref=source, dst_ref=target, send_sem=send, recv_sem=recv,
            device_id=other, device_id_type=MESH,
        )

    def ring_copy(n, way):
        hop = n // KVHEADS
        g = (n + way * (KVHEADS // 2)) % KVHEADS
        if way == 0:
            source, target = hop, hop + 1
        else:
            source = jnp.where(hop == 0, 0, hop + HOPS)
            target = jnp.where(hop == HOPS - 1, HOPS, hop + HOPS + 1)
        return copy(
            kv.at[source, g], kv.at[target, g], y_send.at[way, n], y_recv.at[way, n], rings[way]
        )

    cosine, sine = long_cos[...], long_sin[...]
    for g in range(KVHEADS):
        kv[0, g, :, :HEAD_DIM] = rotated(
            k_long[:, g * HEAD_DIM : (g + 1) * HEAD_DIM], cosine, sine
        )
        kv[0, g, :, HEAD_DIM:] = v_long[:, g * HEAD_DIM : (g + 1) * HEAD_DIM]
    for n in range(KVHEADS):
        for way in range(2):
            ring_copy(n, way).start()

    pools = [pool0, pool1]

    def mate_copy(j, g):
        return copy(
            pools[j].at[g], pools[j].at[CHUNKS + g], mate_send.at[j, g], mate_recv.at[j, g], mate
        )

    for j in range(BINS):
        rows = slice(j * BIN_LEN, (j + 1) * BIN_LEN)
        bin_cos, bin_sin = short_cos[rows], short_sin[rows]
        row = lax.broadcasted_iota(jnp.int32, (BIN_LEN, BIN_LEN), 0)
        col = lax.broadcasted_iota(jnp.int32, (BIN_LEN, BIN_LEN), 1)
        allowed = (col >= short_start[rows]) & (col <= row)
        bias = jnp.where(allowed, 0.0, NEGATIVE)
        bias = jnp.concatenate([bias] * GROUP, 0)
        for g in range(CHUNKS):
            lanes = slice(g * HEAD_DIM, (g + 1) * HEAD_DIM)
            heads = turned_heads(q_short, rows, g, bin_cos, bin_sin)
            scores = score(heads, rotated(k_short[rows, lanes], bin_cos, bin_sin)) + bias
            weight = jnp.exp2(scores - jnp.max(scores, axis=1, keepdims=True))
            blended = jnp.dot(
                weight.astype(jnp.bfloat16), v_short[rows, lanes], preferred_element_type=jnp.float32
            )
            blended = blended / jnp.sum(weight, axis=1, keepdims=True)
            pools[j][g] = side_by_side(blended.astype(jnp.bfloat16))
            mate_copy(j, g).start()

    shift = [0] + [-h for h in range(1, HOPS + 1)] + [h for h in range(1, NY - HOPS)]
    row = lax.broadcasted_iota(jnp.int32, (span, span), 0) + ctx * span
    col = lax.broadcasted_iota(jnp.int32, (span, span), 1)
    for i in range(NY):
        key_index = col + (ctx + NY + shift[i]) % NY * span
        allowed = (key_index >= long_start[...]) & (key_index <= row)
        bias_ref[i] = jnp.where(allowed, 0.0, NEGATIVE)

    def attend(g, blocks):
        first, last = 0 in blocks, HOPS in blocks
        if first:
            query[g] = turned_heads(q_long, slice(None), g, long_cos[...], long_sin[...])
        keys = jnp.concatenate([kv[i, g, :, :HEAD_DIM] for i in blocks], 0)
        values = jnp.concatenate([kv[i, g, :, HEAD_DIM:] for i in blocks], 0)
        bias = jnp.concatenate([bias_ref[i] for i in blocks], 1)
        for i in range(GROUP):
            part = pl.ds(i * span, span)
            scores = score(query[g, part], keys) + bias
            peak = jnp.max(scores, axis=1, keepdims=True)
            if not first:
                old = top[g, part]
                peak = jnp.maximum(peak, old[:, :1])
            weight = jnp.exp2(scores - peak)
            amount = jnp.sum(weight, axis=1, keepdims=True)
            blended = jnp.dot(
                weight.astype(jnp.bfloat16), values, preferred_element_type=jnp.float32
            )
            if not first:
                shrink = jnp.exp2(old[:, :1] - peak)
                amount = amount + total[g, part][:, :1] * shrink
                blended = blended + acc[g, part] * shrink
            if last:
                out_long[:, columns(g * GROUP + i, HEAD_DIM)] = (blended / amount).astype(
                    jnp.bfloat16
                )
            else:
                top[g, part] = jnp.broadcast_to(peak, (span, HEAD_DIM))
                total[g, part] = jnp.broadcast_to(amount, (span, HEAD_DIM))
                acc[g, part] = blended

    near = [0, 1, HOPS + 1]
    middle = [2, HOPS + 2]
    far = [3, HOPS, HOPS + 3]

    def route_copy(slot, d):
        return copy(
            stage.at[slot, d], landing.at[slot, d], route_send.at[slot, d], route_recv.at[slot, d],
            routes[d],
        )

    def entry(j, place):
        index = route_ref[j, place]
        return index + jnp.where(index < CHUNKS, order_ref[1 + j], 0)

    def collect(j, step):
        slot = BINS * step + j
        for d in range(DIRS):
            route_copy(slot, d).wait_recv()
            pools[j][OWN + DIRS * step + d] = landing[slot, d]

    def send(j, step):
        slot = BINS * step + j
        for d in range(DIRS):
            stage[slot, d] = pools[j][entry(j, step * DIRS + d)]
            route_copy(slot, d).start()

    def ring(n):
        for way in range(2):
            ring_copy(n, way).wait_recv()

        @pl.when(n + KVHEADS < Y_SENDS)
        def _():
            for way in range(2):
                ring_copy(n + KVHEADS, way).start()

    for j in range(BINS):
        for g in range(CHUNKS):
            mate_copy(j, g).wait_recv()
        send(j, 0)
        ring(j)

    def pair(step, work):
        for j in range(BINS):
            collect(j, step - 1)
            send(j, step)
            ring(BINS * step + j)
            work(BINS * step + j)

    @pl.loop(1, 2)
    def _(step):
        pair(step, lambda n: None)

    @pl.loop(2, 4)
    def _(step):
        pair(step, lambda n: attend(n - 4, near))

    @pl.loop(4, 6)
    def _(step):
        pair(step, lambda n: attend(n - 8, middle))

    @pl.loop(6, 7)
    def _(step):
        def work(n):
            attend(n - 12, far)
            attend(n - 10, far)

        pair(step, work)

    for j in range(BINS):
        collect(j, STEPS - 2)
        send(j, STEPS - 1)
    for j in range(BINS):
        collect(j, STEPS - 1)

    swap = order_ref[0]
    for g in range(CHUNKS):
        chunk0 = pool0[entry(0, DIRS * STEPS + g)]
        chunk1 = pool1[entry(1, DIRS * STEPS + g)]
        lanes = slice(g * WIDE, (g + 1) * WIDE)
        out_short[:BIN_LEN, lanes] = jnp.where(swap == 0, chunk0, chunk1)
        out_short[BIN_LEN:, lanes] = jnp.where(swap == 0, chunk1, chunk0)

    for j in range(BINS):
        for g in range(CHUNKS):
            mate_copy(j, g).wait_send()

    @pl.loop(0, BINS * STEPS)
    def _(slot):
        for d in range(DIRS):
            route_copy(slot, d).wait_send()

    @pl.loop(0, Y_SENDS)
    def _(n):
        for way in range(2):
            ring_copy(n, way).wait_send()


VMEM = pl.BlockSpec(memory_space=pltpu.VMEM)
SMEM = pl.BlockSpec(memory_space=pltpu.SMEM)


def local(q_short, k_short, v_short, short_lengths, bin_dest, q_long, k_long, v_long, long_lengths):
    dp_index = lax.axis_index("dp")
    ctx_index = lax.axis_index("ctx")
    span = q_long.shape[0]

    my_rows = ctx_index * span + jnp.arange(span, dtype=jnp.int32)
    my_start = doc_start(long_lengths[0], my_rows)
    long_cos, long_sin = turn_tables(my_rows - my_start)

    home = lax.dynamic_index_in_dim(short_lengths[:, 0], dp_index, 0, keepdims=False)
    token = jnp.arange(BIN_LEN, dtype=jnp.int32)[None, :]
    start = doc_start(home, token)
    short_cos, short_sin = turn_tables((token - start).reshape(-1))

    masks = bin_dest[0, 0]
    route = jnp.asarray(route_table())[masks // 2, dp_index // 2]
    swap = ((dp_index ^ masks[0]) > (dp_index ^ masks[1])).astype(jnp.int32)
    order = jnp.concatenate([swap[None], masks % 2 * CHUNKS])

    bf16, f32 = jnp.bfloat16, jnp.float32
    slots = BINS * STEPS
    dma = pltpu.SemaphoreType.DMA
    out_short, out_long = pl.pallas_call(
        kernel,
        out_shape=[jax.ShapeDtypeStruct(q_short.shape, bf16), jax.ShapeDtypeStruct(q_long.shape, bf16)],
        in_specs=[SMEM, SMEM] + [VMEM] * 12,
        out_specs=[VMEM, VMEM],
        scratch_shapes=[
            pltpu.VMEM((POOL, BIN_LEN, WIDE), bf16),
            pltpu.VMEM((POOL, BIN_LEN, WIDE), bf16),
            pltpu.VMEM((slots, DIRS, BIN_LEN, WIDE), bf16),
            pltpu.VMEM((slots, DIRS, BIN_LEN, WIDE), bf16),
            pltpu.VMEM((NY, KVHEADS, span, 2 * HEAD_DIM), bf16),
            pltpu.VMEM((KVHEADS, GROUP * span, HEAD_DIM), bf16),
            pltpu.VMEM((KVHEADS, GROUP * span, HEAD_DIM), f32),
            pltpu.VMEM((KVHEADS, GROUP * span, HEAD_DIM), f32),
            pltpu.VMEM((KVHEADS, GROUP * span, HEAD_DIM), f32),
            pltpu.VMEM((NY, span, span), f32),
            dma((BINS, CHUNKS)),
            dma((BINS, CHUNKS)),
            dma((slots, DIRS)),
            dma((slots, DIRS)),
            dma((2, Y_SENDS)),
            dma((2, Y_SENDS)),
        ],
        compiler_params=pltpu.CompilerParams(
            collective_id=0, has_side_effects=True, vmem_limit_bytes=48 * 2**20
        ),
    )(
        route, order, q_short, k_short, v_short, short_cos, short_sin, start.reshape(-1)[:, None],
        q_long, k_long, v_long, long_cos, long_sin, my_start[:, None],
    )
    return (out_short, out_long)


def solution(mesh):
    in_specs = (
        P(("dp", "ctx"), None),
        P(("dp", "ctx"), None),
        P(("dp", "ctx"), None),
        P(None, "ctx", None, None),
        P(None, "ctx", None),
        P(("dp", "ctx"), None),
        P(("dp", "ctx"), None),
        P(("dp", "ctx"), None),
        P("dp", None),
    )
    out_specs = (P(("dp", "ctx"), None), P(("dp", "ctx"), None))
    return jax.shard_map(local, mesh=mesh, in_specs=in_specs, out_specs=out_specs, check_vma=False)
```

time: 188 us -> 68 us (0.36)
  the two profiles are of different devices: /device:TPU:1 before, /device:TPU:24 now
where the time goes in v1:
time: 68 us; the launch traced here: 67.7 us
  Pallas kernels  54.8 us (81%)
  local copies, waits for them, and re-layouts  6.91 us (10%)
  between operations  3.48 us (5%)
  other arithmetic  2.47 us (4%)
    pallas_call x1, Pallas kernels, local(): pl.pallas_call(kernel, out_shape=[jax.ShapeDtypeStruct(q_short.shape, bf1...  54.8 us
    unnamed x20, local copies, waits for them, and re-layouts  3.28 us
    gather x1, local copies, waits for them, and re-layouts, local(): route = jnp.asarray(route_table())[masks // 2, dp_index // 2]  1.45 us

profile of v1, /device:TPU:24, one launch (start us, length us, event | category | flops | bytes accessed | tf_op | source)
XLA Modules:
  0.0 67.7 jit_solution(5928441137518581071)
XLA Ops:
  0.6 0.0 copy-start
  0.7 0.0 copy-start.8
  0.7 0.7 copy-done.8
  1.3 0.1 slice_reduce_fusion
  1.5 1.4 %gather_fusion = s32[2,36]{1,0:T(2,128)S(1)} fusion(s32[32,32,36]{2,1,0:T(8,128)} %constant.65.clone, s32[2]{0:T(128)S(1)} %fusion.12), kind=kCustom, calls=%fused_computation | custom fusion | bytes 592 | tf_op jit(solution)/shard_map/gather | solution.py:360
  3.0 0.0 copy-start.7
  3.0 0.1 sub.49
  3.1 0.6 copy-done.7
  3.6 0.6 fusion.15
  5.5 0.7 %fusion.7 = f32[128]{0:T(128)S(1)} fusion(s32[]{:T(128)} %bitcast.6, s32[]{:T(128)} %bitcast.5, s32[]{:T(128)S(6)} %mul.47), kind=kLoop, calls=%fused_computation.35 | loop fusion | flops 896 | bytes 524 | tf_op jit(solution)/shard_map/convert_element_type | solution.py:95
  6.2 0.5 fusion.14
  8.1 0.1 pad_add_fusion.order_ref
  8.1 0.0 copy-done
  8.1 0.1 constant_dynamic-slice_fusion
  8.2 0.1 copy.19
  8.3 0.2 slice_reduce_fusion.1
  8.5 0.1 ge.113
  8.6 0.1 ge.114
  8.6 0.1 ge.109
  8.7 0.1 ge.110
  8.8 0.0 copy-start.6
  8.8 0.1 ge.130
  9.0 0.1 ge.131
  9.1 0.0 copy-start.5
  9.1 0.1 sub.54
  9.3 0.0 copy-start.3
  9.3 0.0 copy-start.4
  9.3 0.7 %compare_select_fusion.1 = (s32[128,1]{1,0:T(8,128)S(1)}, s32[128,1]{1,0:T(8,128)S(1)}) fusion(s32[128,1]{1,0:T(8,128)S(1)} %ge.130, s32[128,1]{1,0:T(8,128)S(1)} %sub.54, s32[128,1]{1,0:T(8,128)S(1)} %ge.131, s32[]{:T(128)} %bitcast.6, s32[]{:T(128)} %bitcast.5, s32[]{:T(128)S(6)} %mul.47), kind=kLoop, calls=%fused_computation.2 | loop fusion | flops 1152 | bytes 2572 | tf_op jit(solution)/shard_map/jit(_where)/select_n | solution.py:90
  10.0 0.0 copy-start.1
  10.1 0.0 copy-start.2
  10.1 0.5 fusion.3
  10.6 0.1 pad_maximum_fusion.2
  10.7 0.1 pad_maximum_fusion
  10.8 0.0 copy-done.6
  10.8 0.0 copy-done.5
  10.8 0.0 copy-done.3
  10.9 0.0 copy-done.4
  10.9 0.3 copy-done.1
  11.1 0.2 copy-done.2
  11.3 54.8 %shard_map.113 = (bf16[128,2048]{1,0:T(8,128)(2,1)S(1)}, bf16[128,2048]{1,0:T(8,128)(2,1)S(1)}) custom-call(s32[2,36]{1,0:T(2,128)S(1)} %gather_fusion, s32[3]{0:T(128)S(1)} %pad_add_fusion.order_ref, bf16[128,2048]{1,0:T(8,128)(2,1)S(1)} %copy-done.1, bf16[128,512]{1,0:T(8,128)(2,1)S(1)} %copy-done.3, bf16[128,512]{1,0:T(8,128)(2,1)S(1)} %copy-done.4, ...), custom_call_target="tpu_custom_call" | custom-call | tf_op jit(solution)/shard_map/pallas_call | solution.py:367
  66.1 0.8 %copy.28 = bf16[128,2048]{1,0:T(8,128)(2,1)} copy(bf16[128,2048]{1,0:T(8,128)(2,1)S(1)} %get-tuple-element.25) | data formatting | bytes 1048576
  66.9 0.8 %copy.29 = bf16[128,2048]{1,0:T(8,128)(2,1)} copy(bf16[128,2048]{1,0:T(8,128)(2,1)S(1)} %get-tuple-element.26) | data formatting | bytes 1048576
  (6 shorter events, 0.1 us)
Async XLA Ops:
  0.6 7.5 %copy-start = (s32[64,1,2,3]{0,2,3,1:T(2,128)S(1)}, s32[64,1,2,3]{0,2,3,1:T(2,128)}, u32[]{:S(2)}) copy-start(s32[64,1,2,3]{0,2,3,1:T(2,128)} %param.13) | copy-start | bytes 4612
  0.7 0.7 %copy-start.8 = (s32[64,1,2]{0,2,1:T(2,128)S(1)}, s32[64,1,2]{0,2,1:T(2,128)}, u32[]{:S(2)}) copy-start(s32[64,1,2]{0,2,1:T(2,128)} %param.14) | copy-start | bytes 1540
  3.0 0.7 copy-start.7
  8.8 2.0 %copy-start.6 = (bf16[128,512]{1,0:T(8,128)(2,1)S(1)}, bf16[128,512]{1,0:T(8,128)(2,1)}, u32[]{:S(2)}) copy-start(bf16[128,512]{1,0:T(8,128)(2,1)} %v_long.1) | copy-start | bytes 393220
  9.1 1.7 %copy-start.5 = (bf16[128,512]{1,0:T(8,128)(2,1)S(1)}, bf16[128,512]{1,0:T(8,128)(2,1)}, u32[]{:S(2)}) copy-start(bf16[128,512]{1,0:T(8,128)(2,1)} %k_long.1) | copy-start | bytes 393220
  9.3 1.6 %copy-start.3 = (bf16[128,512]{1,0:T(8,128)(2,1)S(1)}, bf16[128,512]{1,0:T(8,128)(2,1)}, u32[]{:S(2)}) copy-start(bf16[128,512]{1,0:T(8,128)(2,1)} %k_short.1) | copy-start | bytes 393220
  9.3 1.6 %copy-start.4 = (bf16[128,512]{1,0:T(8,128)(2,1)S(1)}, bf16[128,512]{1,0:T(8,128)(2,1)}, u32[]{:S(2)}) copy-start(bf16[128,512]{1,0:T(8,128)(2,1)} %v_short.1) | copy-start | bytes 393220
  10.0 1.1 %copy-start.1 = (bf16[128,2048]{1,0:T(8,128)(2,1)S(1)}, bf16[128,2048]{1,0:T(8,128)(2,1)}, u32[]{:S(2)}) copy-start(bf16[128,2048]{1,0:T(8,128)(2,1)} %q_short.1) | copy-start | bytes 1572868
  10.1 1.2 %copy-start.2 = (bf16[128,2048]{1,0:T(8,128)(2,1)S(1)}, bf16[128,2048]{1,0:T(8,128)(2,1)}, u32[]{:S(2)}) copy-start(bf16[128,2048]{1,0:T(8,128)(2,1)} %q_long.1) | copy-start | bytes 1572868

commit v2 on v1

v2 whole, which is shorter than its diff:
```python
import functools
import math

import jax
import jax.numpy as jnp
import numpy as np
from jax import lax
from jax.experimental import pallas as pl
from jax.experimental.pallas import tpu as pltpu
from jax.sharding import PartitionSpec as P

QHEADS = 16
KVHEADS = 4
GROUP = QHEADS // KVHEADS
HEAD_DIM = 128
HALF = HEAD_DIM // 2
WIDE = GROUP * HEAD_DIM
BIN_LEN = 64
BINS = 2
THETA = 500000.0
NEGATIVE = -1e30
SCALE = math.log2(math.e) / math.sqrt(HEAD_DIM)

NZ, NX, NY = 8, 4, 8
HALVES = 2
PART = WIDE // HALVES
CHUNKS = KVHEADS
STEPS = 8
DIRS = 4
OWN = 2 * CHUNKS
POOL = OWN + DIRS * STEPS
ROUTE = 64
HOPS = NY // 2
Y_SENDS = 3 * KVHEADS + KVHEADS // 2
MESH = pl.DeviceIdType.MESH


def moved(place, direction):
    z, x = divmod(place, NX)
    if direction < 2:
        x = (x + (1, -1)[direction]) % NX
    else:
        z = (z + (1, -1)[direction - 2]) % NZ
    return z * NX + x


@functools.cache
def route_table():
    table = np.zeros((NZ * NX, NZ * NX, ROUTE), np.int32)
    for mask in range(NZ * NX):
        packets = []
        for place in range(NZ * NX):
            z, x = divmod(place, NX)
            goal_z, goal_x = divmod(place ^ mask, NX)
            for chunk in range(CHUNKS):
                dz, dx = (goal_z - z) % NZ, (goal_x - x) % NX
                if dz > NZ // 2 or (dz == NZ // 2 and chunk % 2):
                    dz -= NZ
                if dx > NX // 2 or (dx == NX // 2 and (chunk // (2 if mask // NX == NZ // 2 else 1)) % 2):
                    dx -= NX
                packets.append([place, dz, dx, chunk, chunk])
        step = 0
        while any(p[1] or p[2] for p in packets):
            order = sorted(packets, key=lambda p: (-abs(p[1]) - abs(p[2]), -abs(p[1]), p[4]))
            taken, moves = set(), []
            for p in order:
                options = []
                if p[1]:
                    options.append(2 if p[1] > 0 else 3)
                if p[2]:
                    options.append(0 if p[2] > 0 else 1)
                for d in options:
                    if (p[0], d) not in taken:
                        taken.add((p[0], d))
                        moves.append((p, d))
                        break
            for p, d in moves:
                table[mask, p[0], step * DIRS + d] = p[3]
                p[0] = moved(p[0], d)
                p[2 if d < 2 else 1] -= (1, -1)[d % 2]
                p[3] = OWN + DIRS * step + d
            step += 1
        assert step <= STEPS
        for p in packets:
            table[mask, p[0], DIRS * STEPS + p[4]] = p[3]
    return np.ascontiguousarray(table.transpose(1, 0, 2)).reshape(-1)


INVERSE = np.power(THETA, -np.arange(HALF, dtype=np.float64) * (2.0 / HEAD_DIM)).astype(np.float32)
QUARTER1 = float(np.float32(1.5703125))
QUARTER2 = float(np.float32(math.floor((math.pi / 2 - QUARTER1) * 2**23) / 2**23))
QUARTER3 = float(np.float32(math.pi / 2 - QUARTER1 - QUARTER2))


def turns(angle):
    quarters = jnp.floor(angle * (2.0 / math.pi) + 0.5)
    r = ((angle - quarters * QUARTER1) - quarters * QUARTER2) - quarters * QUARTER3
    s = r * r
    sine = 1.0 / 362880
    for k in (-1.0 / 5040, 1.0 / 120, -1.0 / 6):
        sine = sine * s + k
    sine = r + r * s * sine
    cosine = 1.0 / 40320
    for k in (-1.0 / 720, 1.0 / 24, -0.5, 1.0):
        cosine = cosine * s + k
    count = quarters.astype(jnp.int32)
    odd, turned = (count & 1) == 1, (count & 2) == 2
    first, second = jnp.where(odd, sine, cosine), jnp.where(odd, cosine, sine)
    flip = turned != odd
    return jnp.where(flip, -first, first), jnp.where(turned, -second, second)


def doc_start(first, second, index):
    return jnp.where(index >= second, second, jnp.where(index >= first, first, 0))


def rotated(block, cosine, sine):
    wide = block.astype(jnp.float32)
    return (wide * cosine + pltpu.roll(wide, HALF, 1) * sine).astype(jnp.bfloat16)


def lanes(i, width):
    return slice(i * width, (i + 1) * width)


def stacked_heads(q_ref, g, cosine, sine):
    heads = range(g * GROUP, (g + 1) * GROUP)
    return jnp.concatenate([rotated(q_ref[:, lanes(h, HEAD_DIM)], cosine, sine) for h in heads], 0)


def score(query, key):
    return SCALE * lax.dot_general(
        query, key, (((1,), (1,)), ((), ())), preferred_element_type=jnp.float32
    )


def blend(weight, values):
    wide = jnp.concatenate([values, jnp.ones_like(values)], 1)
    return jnp.dot(weight.astype(jnp.bfloat16), wide, preferred_element_type=jnp.float32)


def kernel(
    table_any, inverse_any, lengths_any, dest_any, long_lengths_any,
    k_long_any, v_long_any, q_short_any, k_short_any, v_short_any, q_long_any,
    out_short, out_long,
    table, dest, inverse, lengths, long_lengths,
    k_long, v_long, q_short, k_short, v_short, q_long,
    pool00, pool01, pool10, pool11, stage, landing, kv, query, top, acc, bias_ref,
    load_sem, mate_send, mate_recv, route_send, route_recv, y_send, y_recv,
):
    dp, ctx = lax.axis_index("dp"), lax.axis_index("ctx")
    core, x, z = dp % 2, (dp // 2) % NX, dp // (2 * NX)
    span = q_long.shape[0]

    loads = [
        (table_any.at[pl.ds(pl.multiple_of((dp // 2) * (NZ * NX * ROUTE), NZ * NX * ROUTE), NZ * NX * ROUTE)], table),
        (dest_any, dest),
        (inverse_any, inverse),
        (lengths_any, lengths),
        (long_lengths_any, long_lengths),
        (k_long_any, k_long),
        (v_long_any, v_long),
        (q_short_any, q_short),
        (k_short_any, k_short),
        (v_short_any, v_short),
        (q_long_any, q_long),
    ]
    loads = [pltpu.make_async_copy(a, b, load_sem.at[i]) for i, (a, b) in enumerate(loads)]
    for load in loads[2:] + loads[:2]:
        load.start()

    def at(z_to, x_to):
        return (((z_to + NZ) % NZ * NX + (x_to + NX) % NX) * 2 + core, ctx)

    mate = (dp + 1 - 2 * core, ctx)
    routes = [at(z, x + 1), at(z, x - 1), at(z + 1, x), at(z - 1, x)]
    rings = [(dp, (ctx + 1) % NY), (dp, (ctx + NY - 1) % NY)]

    barrier = pltpu.get_barrier_semaphore()
    for other in [mate, *routes, *rings]:
        pl.semaphore_signal(barrier, inc=1, device_id=other, device_id_type=MESH)

    def copy(source, target, send, recv, other):
        return pltpu.make_async_remote_copy(
            src_ref=source, dst_ref=target, send_sem=send, recv_sem=recv,
            device_id=other, device_id_type=MESH,
        )

    def ring_copy(n, way):
        hop = n // KVHEADS
        g = (n + way * (KVHEADS // 2)) % KVHEADS
        if way == 0:
            source, target = hop, hop + 1
        else:
            source = jnp.where(hop == 0, 0, hop + HOPS)
            target = jnp.where(hop == HOPS - 1, HOPS, hop + HOPS + 1)
        return copy(
            kv.at[source, g], kv.at[target, g], y_send.at[way, n], y_recv.at[way, n], rings[way]
        )

    for load in loads[2:5]:
        load.wait()
    row = lax.broadcasted_iota(jnp.int32, (span, HEAD_DIM), 0)
    lane = lax.broadcasted_iota(jnp.int32, (span, HEAD_DIM), 1)
    mine = lax.broadcasted_iota(jnp.int32, lengths.shape[2:], 1) == dp
    home = [jnp.sum(jnp.where(mine, lengths[0, d], 0), axis=1, keepdims=True) for d in range(2)]
    first = jnp.where(row < BIN_LEN, home[0][0:1], home[0][1:2])
    second = first + jnp.where(row < BIN_LEN, home[1][0:1], home[1][1:2])
    token = row % BIN_LEN
    short_start = doc_start(first, second, token)
    my_row = row + ctx * span
    first = long_lengths[:, 0:1]
    long_start = doc_start(first, first + long_lengths[:, 1:2], my_row)
    position = jnp.where(lane < HALF, token - short_start, my_row - long_start)
    cosine, sine = turns(position.astype(jnp.float32) * inverse[...])
    cosine_swap, sine_swap = pltpu.roll(cosine, HALF, 1), pltpu.roll(sine, HALF, 1)
    low = lane < HALF
    short_cos, short_sin = jnp.where(low, cosine, cosine_swap), jnp.where(low, -sine, sine_swap)
    long_cos, long_sin = jnp.where(low, cosine_swap, cosine), jnp.where(low, -sine_swap, sine)

    for load in loads[5:7]:
        load.wait()
    for g in range(KVHEADS):
        kv[0, g, :, :HEAD_DIM] = rotated(k_long[:, lanes(g, HEAD_DIM)], long_cos, long_sin)
        kv[0, g, :, HEAD_DIM:] = v_long[:, lanes(g, HEAD_DIM)]
    pl.semaphore_wait(barrier, 3 + DIRS)
    for n in range(KVHEADS):
        for way in range(2):
            ring_copy(n, way).start()

    pools = [pool00, pool01, pool10, pool11]
    streams = range(BINS * HALVES)

    def mate_copy(t, g):
        return copy(
            pools[t].at[pl.ds(g, 2)], pools[t].at[pl.ds(CHUNKS + g, 2)],
            mate_send.at[t, g // 2], mate_recv.at[t, g // 2], mate,
        )

    for load in loads[7:10]:
        load.wait()
    allowed = (lane >= short_start + (row - token)) & (lane <= row)
    bias = jnp.where(allowed, 0.0, NEGATIVE)
    bias = jnp.concatenate([bias] * GROUP, 0)
    for g in range(CHUNKS):
        heads = stacked_heads(q_short, g, short_cos, short_sin)
        keys = rotated(k_short[:, lanes(g, HEAD_DIM)], short_cos, short_sin)
        scores = score(heads, keys) + bias
        weight = jnp.exp2(scores - jnp.max(scores, axis=1, keepdims=True))
        blended = blend(weight, v_short[:, lanes(g, HEAD_DIM)])
        result = (blended[:, :HEAD_DIM] / blended[:, HEAD_DIM:]).astype(jnp.bfloat16)
        for j in range(BINS):
            for h in range(HALVES):
                parts = [2 * h * span + j * BIN_LEN, (2 * h + 1) * span + j * BIN_LEN]
                pools[j * HALVES + h][g] = jnp.concatenate(
                    [result[p : p + BIN_LEN] for p in parts], 1
                )
        if g % 2:
            for t in streams:
                mate_copy(t, g - 1).start()

    for load in loads[:2]:
        load.wait()
    masks = [dest[0, j, 0] for j in range(BINS)]

    def entry(t, place):
        mask = masks[t // HALVES]
        index = table[(mask >> 1) * ROUTE + place]
        return index + jnp.where(index < CHUNKS, (mask & 1) * CHUNKS, 0)

    def route_copy(slot, d):
        return copy(
            stage.at[slot, d], landing.at[slot, d], route_send.at[slot], route_recv.at[slot], routes[d]
        )

    def all_of(slot):
        return copy(stage.at[slot], landing.at[slot], route_send.at[slot], route_recv.at[slot], routes[0])

    def collect(t, step):
        slot = len(streams) * step + t
        all_of(slot).wait_recv()
        for d in range(DIRS):
            pools[t][OWN + DIRS * step + d] = landing[slot, d]

    def send(t, step):
        slot = len(streams) * step + t
        for d in range(DIRS):
            stage[slot, d] = pools[t][entry(t, step * DIRS + d)]
            route_copy(slot, d).start()

    def ring(n):
        for way in range(2):
            ring_copy(n, way).wait_recv()

        @pl.when(n + KVHEADS < Y_SENDS)
        def _():
            for way in range(2):
                ring_copy(n + KVHEADS, way).start()

    shift = [0] + [-h for h in range(1, HOPS + 1)] + [h for h in range(1, NY - HOPS)]

    def prepare(t):
        query[t] = stacked_heads(q_long, t, long_cos, long_sin)
        for i in (2 * t, 2 * t + 1):
            key_index = lane + (ctx + NY + shift[i]) % NY * span
            allowed = (key_index >= long_start) & (key_index <= my_row)
            bias_ref[i] = jnp.where(allowed, 0.0, NEGATIVE)

    rows = GROUP * span // 2

    def attend(g, half, blocks):
        begins, ends = 0 in blocks, HOPS in blocks
        part = pl.ds(half * rows, rows)
        keys = jnp.concatenate([kv[i, g, :, :HEAD_DIM] for i in blocks], 0)
        values = jnp.concatenate([kv[i, g, :, HEAD_DIM:] for i in blocks], 0)
        bias = jnp.concatenate([bias_ref[i] for i in blocks], 1)
        scores = score(query[g, part], keys) + jnp.concatenate([bias] * (GROUP // 2), 0)
        peak = jnp.max(scores, axis=1, keepdims=True)
        if not begins:
            old = top[g, part]
            peak = jnp.maximum(peak, old[:, :1])
        blended = blend(jnp.exp2(scores - peak), values)
        if not begins:
            blended = blended + acc[g, part] * jnp.exp2(old[:, :1] - peak)
        if ends:
            result = (blended[:, :HEAD_DIM] / blended[:, HEAD_DIM:]).astype(jnp.bfloat16)
            result = jnp.concatenate([result[i * span : (i + 1) * span] for i in range(GROUP // 2)], 1)
            width = GROUP // 2 * HEAD_DIM
            out_long[:, pl.ds(pl.multiple_of((g * 2 + half) * width, width), width)] = result
        else:
            top[g, part] = jnp.broadcast_to(peak, (rows, HEAD_DIM))
            acc[g, part] = blended

    near = [0, 1, HOPS + 1]
    middle = [2, HOPS + 2]
    far = [3, HOPS, HOPS + 3]

    def one_step(step, work, with_ring=True):
        for t in streams:
            collect(t, step - 1)
            send(t, step)
            if t % 2 == 0 and with_ring:
                ring(BINS * step + t // 2)
            work(t)
            all_of(len(streams) * (step - 1) + t).wait_send()

    loads[10].wait()
    for t in streams:
        for g in (0, 2):
            mate_copy(t, g).wait()
        send(t, 0)
        if t % 2 == 0:
            ring(t // 2)
        prepare(t)

    @pl.loop(1, 2)
    def _(step):
        one_step(step, lambda t: None)

    def unit(step, t, blocks):
        u = len(streams) * step + t
        attend(u // 2, u % 2, blocks)

    @pl.loop(2, 4)
    def _(step):
        one_step(step, lambda t: unit(step - 2, t, near))

    @pl.loop(4, 6)
    def _(step):
        one_step(step, lambda t: unit(step - 4, t, middle))

    one_step(6, lambda t: attend([0, 0, 2, 2][t], t % 2, far))
    one_step(7, lambda t: attend([1, 1, 3, 3][t], t % 2, far), False)

    for t in streams:
        collect(t, STEPS - 1)
    swap = (dp ^ masks[0]) > (dp ^ masks[1])
    for h in range(HALVES):
        for g in range(CHUNKS):
            chunk0 = pools[h][entry(h, DIRS * STEPS + g)]
            chunk1 = pools[HALVES + h][entry(HALVES + h, DIRS * STEPS + g)]
            part = lanes(g * HALVES + h, PART)
            out_short[:BIN_LEN, part] = jnp.where(swap, chunk1, chunk0)
            out_short[BIN_LEN:, part] = jnp.where(swap, chunk0, chunk1)

    for t in streams:
        all_of(len(streams) * (STEPS - 1) + t).wait_send()

    @pl.loop(0, Y_SENDS)
    def _(n):
        for way in range(2):
            ring_copy(n, way).wait_send()


VMEM = pl.BlockSpec(memory_space=pltpu.VMEM)
ANY = pl.BlockSpec(memory_space=pl.ANY)


def local(q_short, k_short, v_short, short_lengths, bin_dest, q_long, k_long, v_long, long_lengths):
    span = q_long.shape[0]
    table = jnp.asarray(route_table())
    inverse = jnp.asarray(np.concatenate([INVERSE, INVERSE])[None, :])
    lengths = jnp.transpose(short_lengths, (1, 3, 2, 0))
    dest = jnp.transpose(bin_dest, (1, 2, 0))

    bf16, f32, i32 = jnp.bfloat16, jnp.float32, jnp.int32
    slots = BINS * HALVES * STEPS
    dma = pltpu.SemaphoreType.DMA
    inputs = [k_long, v_long, q_short, k_short, v_short, q_long]
    out_short, out_long = pl.pallas_call(
        kernel,
        out_shape=[jax.ShapeDtypeStruct(q_short.shape, bf16), jax.ShapeDtypeStruct(q_long.shape, bf16)],
        in_specs=[ANY] * 11,
        out_specs=[VMEM, VMEM],
        scratch_shapes=[
            pltpu.SMEM((NZ * NX * ROUTE,), i32),
            pltpu.SMEM(dest.shape, i32),
            pltpu.VMEM(inverse.shape, f32),
            pltpu.VMEM(lengths.shape, i32),
            pltpu.VMEM(long_lengths.shape, i32),
            *[pltpu.VMEM(a.shape, bf16) for a in inputs],
            *[pltpu.VMEM((POOL, BIN_LEN, PART), bf16)] * (BINS * HALVES),
            pltpu.VMEM((slots, DIRS, BIN_LEN, PART), bf16),
            pltpu.VMEM((slots, DIRS, BIN_LEN, PART), bf16),
            pltpu.VMEM((NY, KVHEADS, span, 2 * HEAD_DIM), bf16),
            pltpu.VMEM((KVHEADS, GROUP * span, HEAD_DIM), bf16),
            pltpu.VMEM((KVHEADS, GROUP * span, HEAD_DIM), f32),
            pltpu.VMEM((KVHEADS, GROUP * span, 2 * HEAD_DIM), f32),
            pltpu.VMEM((NY, span, span), f32),
            dma((11,)),
            dma((BINS * HALVES, CHUNKS // 2)),
            dma((BINS * HALVES, CHUNKS // 2)),
            dma((slots,)),
            dma((slots,)),
            dma((2, Y_SENDS)),
            dma((2, Y_SENDS)),
        ],
        compiler_params=pltpu.CompilerParams(
            collective_id=0, has_side_effects=True, vmem_limit_bytes=56 * 2**20
        ),
    )(table, inverse, lengths, dest, long_lengths, *inputs)
    return (out_short, out_long)


def solution(mesh):
    in_specs = (
        P(("dp", "ctx"), None),
        P(("dp", "ctx"), None),
        P(("dp", "ctx"), None),
        P(None, "ctx", None, None),
        P(None, "ctx", None),
        P(("dp", "ctx"), None),
        P(("dp", "ctx"), None),
        P(("dp", "ctx"), None),
        P("dp", None),
    )
    out_specs = (P(("dp", "ctx"), None), P(("dp", "ctx"), None))
    return jax.shard_map(local, mesh=mesh, in_specs=in_specs, out_specs=out_specs, check_vma=False)
```

time: 68 us -> 53.7 us (0.79)
  the two profiles are of different devices: /device:TPU:24 before, /device:TPU:2 now
where the time goes in v2:
time: 53.7 us; the launch traced here: 53.6 us
  Pallas kernels  50.2 us (93%)
  local copies, waits for them, and re-layouts  2.74 us (5%)
  between operations  0.65 us (1%)
    pallas_call x1, Pallas kernels, local(): pl.pallas_call(kernel, out_shape=[jax.ShapeDtypeStruct(q_short.shape, bf1...  50.2 us
    unnamed x4, local copies, waits for them, and re-layouts  2.74 us

profile of v2, /device:TPU:2, one launch (start us, length us, event | category | flops | bytes accessed | tf_op | source)
XLA Modules:
  0.0 53.6 jit_solution(10672510027157381118)
XLA Ops:
  0.6 50.2 %shard_map.122 = (bf16[128,2048]{1,0:T(8,128)(2,1)}, bf16[128,2048]{1,0:T(8,128)(2,1)}) custom-call(s32[65536]{0:T(1024)} %constant.4.clone.table_any, f32[1,128]{1,0:T(1,128)} %constant.5.clone.inverse_any, s32[1,3,2,64]{3,2,1,0:T(2,128)} %bitcast.2, s32[1,2,64]{2,1,0:T(2,128)} %bitcast.3, s32[1,3]{1,0:T(1,128)} %long_lengths_any.1, ...), custom_call_target="tpu_custom_call" | custom-call | tf_op jit(solution)/shard_map/pallas_call | solution.py:410
  50.8 0.0 copy-start
  50.8 1.9 %copy.15 = bf16[128,2048]{1,0:T(8,128)(2,1)} copy(bf16[128,2048]{1,0:T(8,128)(2,1)} %get-tuple-element.4) | data formatting | bytes 1048576
  52.8 0.0 copy-done
  52.8 0.8 %copy.16 = bf16[128,2048]{1,0:T(8,128)(2,1)} copy(bf16[128,2048]{1,0:T(8,128)(2,1)S(1)} %copy-done) | data formatting | bytes 1048576
Async XLA Ops:
  50.8 2.0 %copy-start = (bf16[128,2048]{1,0:T(8,128)(2,1)S(1)}, bf16[128,2048]{1,0:T(8,128)(2,1)}, u32[]{:S(2)}) copy-start(bf16[128,2048]{1,0:T(8,128)(2,1)} %get-tuple-element.5) | copy-start | bytes 1572868

commit v3 on v2

--- a/solution.py
+++ b/solution.py
@@ -22,13 +22,16 @@
 SCALE = math.log2(math.e) / math.sqrt(HEAD_DIM)
 
 NZ, NX, NY = 8, 4, 8
-HALVES = 2
-PART = WIDE // HALVES
+HALVES = 1
+EARLY = BIN_LEN // 2
+ROWS = EARLY // HALVES
+CUTS = (0, HEAD_DIM, 2 * HEAD_DIM, 4 * HEAD_DIM, 5 * HEAD_DIM)
 CHUNKS = KVHEADS
 STEPS = 8
 DIRS = 4
 OWN = 2 * CHUNKS
 POOL = OWN + DIRS * STEPS
+PIECES = 4
 ROUTE = 64
 HOPS = NY // 2
 Y_SENDS = 3 * KVHEADS + KVHEADS // 2
@@ -123,6 +126,10 @@
     return slice(i * width, (i + 1) * width)
 
 
+def lanes_at(i, width):
+    return pl.ds(i * width, width)
+
+
 def stacked_heads(q_ref, g, cosine, sine):
     heads = range(g * GROUP, (g + 1) * GROUP)
     return jnp.concatenate([rotated(q_ref[:, lanes(h, HEAD_DIM)], cosine, sine) for h in heads], 0)
@@ -142,11 +149,11 @@
 def kernel(
     table_any, inverse_any, lengths_any, dest_any, long_lengths_any,
     k_long_any, v_long_any, q_short_any, k_short_any, v_short_any, q_long_any,
-    out_short, out_long,
+    bin_out, long_out,
     table, dest, inverse, lengths, long_lengths,
     k_long, v_long, q_short, k_short, v_short, q_long,
-    pool00, pool01, pool10, pool11, stage, landing, kv, query, top, acc, bias_ref,
-    load_sem, mate_send, mate_recv, route_send, route_recv, y_send, y_recv,
+    pool_refs, stage, landing, kv, query, top, acc, bias_ref, bin_result, long_result,
+    load_sem, out_sem, mate_send, mate_recv, route_send, route_recv, y_send, y_recv,
 ):
     dp, ctx = lax.axis_index("dp"), lax.axis_index("ctx")
     core, x, z = dp % 2, (dp // 2) % NX, dp // (2 * NX)
@@ -228,36 +235,61 @@
         for way in range(2):
             ring_copy(n, way).start()
 
-    pools = [pool00, pool01, pool10, pool11]
+    pools = [*pool_refs]
     streams = range(BINS * HALVES)
 
-    def mate_copy(t, g):
+    def mate_copy(t):
         return copy(
-            pools[t].at[pl.ds(g, 2)], pools[t].at[pl.ds(CHUNKS + g, 2)],
-            mate_send.at[t, g // 2], mate_recv.at[t, g // 2], mate,
+            pools[t].at[pl.ds(0, CHUNKS)], pools[t].at[pl.ds(CHUNKS, CHUNKS)],
+            mate_send.at[t], mate_recv.at[t], mate,
         )
 
     for load in loads[7:10]:
         load.wait()
-    allowed = (lane >= short_start + (row - token)) & (lane <= row)
-    bias = jnp.where(allowed, 0.0, NEGATIVE)
-    bias = jnp.concatenate([bias] * GROUP, 0)
-    for g in range(CHUNKS):
-        heads = stacked_heads(q_short, g, short_cos, short_sin)
-        keys = rotated(k_short[:, lanes(g, HEAD_DIM)], short_cos, short_sin)
-        scores = score(heads, keys) + bias
+
+    def bias_of(rows, reach):
+        index = lane[rows] % reach
+        allowed = (index >= short_start[rows]) & (index <= token[rows])
+        return jnp.concatenate([jnp.where(allowed, 0.0, NEGATIVE)] * GROUP, 0)
+
+    spot = lane[:EARLY]
+    for j in range(BINS):
+        rows = slice(j * BIN_LEN, (j + 1) * BIN_LEN)
+        early = slice(j * BIN_LEN, j * BIN_LEN + EARLY)
+        late = slice(j * BIN_LEN + EARLY, (j + 1) * BIN_LEN)
+        early_bias, late_bias = bias_of(early, EARLY), bias_of(late, BIN_LEN)
+        early_scores, late_scores = [], []
+        for g in range(CHUNKS):
+            heads = [
+                rotated(q_short[rows, lanes(g * GROUP + i, HEAD_DIM)], short_cos[rows], short_sin[rows])
+                for i in range(GROUP)
+            ]
+            key = rotated(k_short[rows, lanes(g, HEAD_DIM)], short_cos[rows], short_sin[rows])
+            first = jnp.concatenate([q[:EARLY] for q in heads], 0)
+            second = jnp.concatenate([q[EARLY:] for q in heads], 0)
+            keys = jnp.concatenate([key[:EARLY]] * GROUP, 0)
+            early_scores.append(score(first, keys) + early_bias)
+            late_scores.append(score(second, jnp.concatenate([key] * 2, 0)) + late_bias)
+        scores = jnp.concatenate(early_scores + late_scores, 0)
         weight = jnp.exp2(scores - jnp.max(scores, axis=1, keepdims=True))
-        blended = blend(weight, v_short[:, lanes(g, HEAD_DIM)])
-        result = (blended[:, :HEAD_DIM] / blended[:, HEAD_DIM:]).astype(jnp.bfloat16)
-        for j in range(BINS):
+        for g in range(CHUNKS):
+            w = [weight[(g * GROUP + i) * EARLY :][:EARLY] for i in range(GROUP)]
+            packed = w[0]
+            for i in range(1, GROUP):
+                packed = jnp.where(spot // EARLY == i, w[i], packed)
+            w = [weight[((CHUNKS + g) * GROUP + i) * EARLY :][:EARLY] for i in range(GROUP)]
+            left = jnp.where(spot < BIN_LEN, w[0], w[1])
+            right = jnp.where(spot < BIN_LEN, w[2], w[3])
+            pieces = [
+                packed.astype(jnp.bfloat16), v_short[early, lanes(g, HEAD_DIM)],
+                jnp.concatenate([left, right], 1).astype(jnp.bfloat16), v_short[late, lanes(g, HEAD_DIM)],
+            ]
             for h in range(HALVES):
-                parts = [2 * h * span + j * BIN_LEN, (2 * h + 1) * span + j * BIN_LEN]
-                pools[j * HALVES + h][g] = jnp.concatenate(
-                    [result[p : p + BIN_LEN] for p in parts], 1
-                )
-        if g % 2:
-            for t in streams:
-                mate_copy(t, g - 1).start()
+                for i, piece in enumerate(pieces):
+                    part = slice(CUTS[i], CUTS[i + 1])
+                    pools[j * HALVES + h][g, :, part] = piece[h * ROWS : (h + 1) * ROWS]
+        for h in range(HALVES):
+            mate_copy(j * HALVES + h).start()
 
     for load in loads[:2]:
         load.wait()
@@ -306,82 +338,100 @@
             allowed = (key_index >= long_start) & (key_index <= my_row)
             bias_ref[i] = jnp.where(allowed, 0.0, NEGATIVE)
 
-    rows = GROUP * span // 2
-
-    def attend(g, half, blocks):
+    def attend(heads, blocks):
         begins, ends = 0 in blocks, HOPS in blocks
-        part = pl.ds(half * rows, rows)
-        keys = jnp.concatenate([kv[i, g, :, :HEAD_DIM] for i in blocks], 0)
-        values = jnp.concatenate([kv[i, g, :, HEAD_DIM:] for i in blocks], 0)
         bias = jnp.concatenate([bias_ref[i] for i in blocks], 1)
-        scores = score(query[g, part], keys) + jnp.concatenate([bias] * (GROUP // 2), 0)
-        peak = jnp.max(scores, axis=1, keepdims=True)
+        bias = jnp.concatenate([bias] * GROUP, 0)
+        keys = [jnp.concatenate([kv[i, g, :, :HEAD_DIM] for i in blocks], 0) for g in heads]
+        values = [jnp.concatenate([kv[i, g, :, HEAD_DIM:] for i in blocks], 0) for g in heads]
+        scores = [score(query[g], k) + bias for g, k in zip(heads, keys)]
+        peaks = [jnp.max(s, axis=1, keepdims=True) for s in scores]
         if not begins:
-            old = top[g, part]
-            peak = jnp.maximum(peak, old[:, :1])
-        blended = blend(jnp.exp2(scores - peak), values)
-        if not begins:
-            blended = blended + acc[g, part] * jnp.exp2(old[:, :1] - peak)
-        if ends:
-            result = (blended[:, :HEAD_DIM] / blended[:, HEAD_DIM:]).astype(jnp.bfloat16)
-            result = jnp.concatenate([result[i * span : (i + 1) * span] for i in range(GROUP // 2)], 1)
-            width = GROUP // 2 * HEAD_DIM
-            out_long[:, pl.ds(pl.multiple_of((g * 2 + half) * width, width), width)] = result
-        else:
-            top[g, part] = jnp.broadcast_to(peak, (rows, HEAD_DIM))
-            acc[g, part] = blended
+            olds = [top[g][:, :1] for g in heads]
+            peaks = [jnp.maximum(peak, old) for peak, old in zip(peaks, olds)]
+        weights = [jnp.exp2(s - peak) for s, peak in zip(scores, peaks)]
+        blended = [blend(w, v) for w, v in zip(weights, values)]
+        for n, g in enumerate(heads):
+            both = blended[n]
+            if not begins:
+                both = both + acc[g] * jnp.exp2(olds[n] - peaks[n])
+            if ends:
+                result = (both[:, :HEAD_DIM] / both[:, HEAD_DIM:]).astype(jnp.bfloat16)
+                for i in range(GROUP):
+                    long_result[:, lanes(g * GROUP + i, HEAD_DIM)] = result[i * span : (i + 1) * span]
+                long_copy(g).start()
+            else:
+                top[g] = jnp.broadcast_to(peaks[n], top.shape[1:])
+                acc[g] = both
+
+    def long_copy(g):
+        return pltpu.make_async_copy(
+            long_result.at[:, lanes_at(g, WIDE)], long_out.at[:, lanes_at(g, WIDE)], out_sem.at[BINS * CHUNKS + g]
+        )
+
+    def bin_copy(m, g):
+        return pltpu.make_async_copy(bin_result.at[m, g], bin_out.at[m, g], out_sem.at[m * CHUNKS + g])
 
     near = [0, 1, HOPS + 1]
     middle = [2, HOPS + 2]
-    far = [3, HOPS, HOPS + 3]
-
-    def one_step(step, work, with_ring=True):
+    third = [3, HOPS + 3]
+    far = [HOPS]
+
+    def one_step(step, work, rings=(True, True)):
         for t in streams:
-            collect(t, step - 1)
+            phase, half = 2 * step + t // HALVES, t % HALVES
+            if not (isinstance(step, int) and step == 0):
+                collect(t, step - 1)
             send(t, step)
-            if t % 2 == 0 and with_ring:
-                ring(BINS * step + t // 2)
-            work(t)
-            all_of(len(streams) * (step - 1) + t).wait_send()
+            if half == 0 and rings[t // HALVES]:
+                ring(phase - 1)
+            work(phase, [half] if HALVES > 1 else [0, 1])
+            if not (isinstance(step, int) and step == 0):
+                all_of(len(streams) * (step - 1) + t).wait_send()
+
+    def preparing(phase, halves):
+        if 0 in halves:
+            prepare(phase)
+
+    def attending(pick, blocks):
+        def work(phase, halves):
+            if 0 in halves:
+                attend(pick(phase), blocks)
+
+        return work
 
     loads[10].wait()
     for t in streams:
-        for g in (0, 2):
-            mate_copy(t, g).wait()
-        send(t, 0)
-        if t % 2 == 0:
-            ring(t // 2)
-        prepare(t)
-
-    @pl.loop(1, 2)
-    def _(step):
-        one_step(step, lambda t: None)
-
-    def unit(step, t, blocks):
-        u = len(streams) * step + t
-        attend(u // 2, u % 2, blocks)
+        mate_copy(t).wait()
+    one_step(0, preparing, (False, True))
+    one_step(1, preparing)
 
     @pl.loop(2, 4)
     def _(step):
-        one_step(step, lambda t: unit(step - 2, t, near))
+        one_step(step, attending(lambda p: [p - 4], near))
 
     @pl.loop(4, 6)
     def _(step):
-        one_step(step, lambda t: unit(step - 4, t, middle))
-
-    one_step(6, lambda t: attend([0, 0, 2, 2][t], t % 2, far))
-    one_step(7, lambda t: attend([1, 1, 3, 3][t], t % 2, far), False)
+        one_step(step, attending(lambda p: [p - 8], middle))
+
+    one_step(6, attending(lambda p: {12: (0, 1), 13: (2, 3)}[p], third))
+    one_step(7, attending(lambda p: {14: (0, 2), 15: (1, 3)}[p], far), (True, False))
 
     for t in streams:
         collect(t, STEPS - 1)
+
     swap = (dp ^ masks[0]) > (dp ^ masks[1])
-    for h in range(HALVES):
-        for g in range(CHUNKS):
-            chunk0 = pools[h][entry(h, DIRS * STEPS + g)]
-            chunk1 = pools[HALVES + h][entry(HALVES + h, DIRS * STEPS + g)]
-            part = lanes(g * HALVES + h, PART)
-            out_short[:BIN_LEN, part] = jnp.where(swap, chunk1, chunk0)
-            out_short[BIN_LEN:, part] = jnp.where(swap, chunk0, chunk1)
+    for g in range(CHUNKS):
+        chunks = [
+            jnp.concatenate(
+                [pools[t][entry(t, DIRS * STEPS + g)] for t in range(j * HALVES, (j + 1) * HALVES)], 0
+            )
+            for j in range(BINS)
+        ]
+        bin_result[0, g] = jnp.where(swap, chunks[1], chunks[0])
+        bin_result[1, g] = jnp.where(swap, chunks[0], chunks[1])
+        for m in range(BINS):
+            bin_copy(m, g).start()
 
     for t in streams:
         all_of(len(streams) * (STEPS - 1) + t).wait_send()
@@ -391,9 +441,71 @@
         for way in range(2):
             ring_copy(n, way).wait_send()
 
-
-VMEM = pl.BlockSpec(memory_space=pltpu.VMEM)
-ANY = pl.BlockSpec(memory_space=pl.ANY)
+    for g in range(CHUNKS):
+        long_copy(g).wait()
+        for m in range(BINS):
+            bin_copy(m, g).wait()
+
+
+def finish(bins_any, long_any, out_short, out_long, bins, short, long, sem_in, sem_out):
+    rows = long.shape[0] // PIECES
+
+    def long_copies(p):
+        part = pl.ds(p * rows, rows)
+        return (
+            pltpu.make_async_copy(long_any.at[part], long.at[part], sem_in.at[BINS + p]),
+            pltpu.make_async_copy(long.at[part], out_long.at[part], sem_out.at[BINS + p]),
+        )
+
+    def short_copies(m):
+        part = pl.ds(m * BIN_LEN, BIN_LEN)
+        return (
+            pltpu.make_async_copy(bins_any.at[m], bins.at[m], sem_in.at[m]),
+            pltpu.make_async_copy(short.at[part], out_short.at[part], sem_out.at[m]),
+        )
+
+    pieces = [short_copies(m) for m in range(BINS)] + [long_copies(p) for p in range(PIECES)]
+    for load, _ in pieces:
+        load.start()
+
+    spot = lax.broadcasted_iota(jnp.int32, (EARLY, HEAD_DIM), 1)
+
+    def chosen(test):
+        return jnp.where(test, 1.0, 0.0).astype(jnp.bfloat16)
+
+    quarter = [chosen(spot // EARLY == i) for i in range(GROUP)]
+    side = [chosen(spot < BIN_LEN), chosen(spot >= BIN_LEN)]
+
+    def finished(weight, values):
+        blended = blend(weight, values)
+        result = (blended[:, :HEAD_DIM] / blended[:, HEAD_DIM:]).astype(jnp.bfloat16)
+        return jnp.concatenate([result[i * EARLY : (i + 1) * EARLY] for i in range(GROUP)], 1)
+
+    for m in range(BINS):
+        pieces[m][0].wait()
+        for g in range(CHUNKS):
+            chunk = bins[m, g]
+            first, first_v, second, second_v = [chunk[:, CUTS[i] : CUTS[i + 1]] for i in range(4)]
+            early = jnp.concatenate([first * q for q in quarter], 0)
+            late = [second[:, lanes(i // 2, HEAD_DIM)] * side[i % 2] for i in range(GROUP)]
+            late = jnp.concatenate(late, 0)
+            start = m * BIN_LEN
+            short[start : start + EARLY, lanes(g, WIDE)] = finished(
+                early, jnp.concatenate([first_v] * GROUP, 0)
+            )
+            short[start + EARLY : start + BIN_LEN, lanes(g, WIDE)] = finished(
+                late, jnp.concatenate([first_v, second_v] * 2, 0)
+            )
+        if m == 0:
+            for load, store in pieces[BINS:]:
+                load.wait()
+                store.start()
+        pieces[m][1].start()
+    for _, store in pieces:
+        store.wait()
+
+
+HBM = pl.BlockSpec(memory_space=pltpu.HBM)
 
 
 def local(q_short, k_short, v_short, short_lengths, bin_dest, q_long, k_long, v_long, long_lengths):
@@ -407,11 +519,12 @@
     slots = BINS * HALVES * STEPS
     dma = pltpu.SemaphoreType.DMA
     inputs = [k_long, v_long, q_short, k_short, v_short, q_long]
-    out_short, out_long = pl.pallas_call(
+    bins_shape = (BINS, CHUNKS, EARLY, CUTS[-1])
+    bins, long = pl.pallas_call(
         kernel,
-        out_shape=[jax.ShapeDtypeStruct(q_short.shape, bf16), jax.ShapeDtypeStruct(q_long.shape, bf16)],
-        in_specs=[ANY] * 11,
-        out_specs=[VMEM, VMEM],
+        out_shape=[jax.ShapeDtypeStruct(bins_shape, bf16), jax.ShapeDtypeStruct(q_long.shape, bf16)],
+        in_specs=[HBM] * 11,
+        out_specs=[HBM, HBM],
         scratch_shapes=[
             pltpu.SMEM((NZ * NX * ROUTE,), i32),
             pltpu.SMEM(dest.shape, i32),
@@ -419,17 +532,20 @@
             pltpu.VMEM(lengths.shape, i32),
             pltpu.VMEM(long_lengths.shape, i32),
             *[pltpu.VMEM(a.shape, bf16) for a in inputs],
-            *[pltpu.VMEM((POOL, BIN_LEN, PART), bf16)] * (BINS * HALVES),
-            pltpu.VMEM((slots, DIRS, BIN_LEN, PART), bf16),
-            pltpu.VMEM((slots, DIRS, BIN_LEN, PART), bf16),
+            [pltpu.VMEM((POOL, ROWS, CUTS[-1]), bf16)] * (BINS * HALVES),
+            pltpu.VMEM((slots, DIRS, ROWS, CUTS[-1]), bf16),
+            pltpu.VMEM((slots, DIRS, ROWS, CUTS[-1]), bf16),
             pltpu.VMEM((NY, KVHEADS, span, 2 * HEAD_DIM), bf16),
             pltpu.VMEM((KVHEADS, GROUP * span, HEAD_DIM), bf16),
             pltpu.VMEM((KVHEADS, GROUP * span, HEAD_DIM), f32),
             pltpu.VMEM((KVHEADS, GROUP * span, 2 * HEAD_DIM), f32),
             pltpu.VMEM((NY, span, span), f32),
+            pltpu.VMEM(bins_shape, bf16),
+            pltpu.VMEM(q_long.shape, bf16),
             dma((11,)),
-            dma((BINS * HALVES, CHUNKS // 2)),
-            dma((BINS * HALVES, CHUNKS // 2)),
+            dma((BINS * CHUNKS + KVHEADS,)),
+            dma((BINS * HALVES,)),
+            dma((BINS * HALVES,)),
             dma((slots,)),
             dma((slots,)),
             dma((2, Y_SENDS)),
@@ -439,7 +555,20 @@
             collective_id=0, has_side_effects=True, vmem_limit_bytes=56 * 2**20
         ),
     )(table, inverse, lengths, dest, long_lengths, *inputs)
-    return (out_short, out_long)
+    return pl.pallas_call(
+        finish,
+        out_shape=[jax.ShapeDtypeStruct(q_short.shape, bf16), jax.ShapeDtypeStruct(q_long.shape, bf16)],
+        in_specs=[HBM, HBM],
+        out_specs=[HBM, HBM],
+        scratch_shapes=[
+            pltpu.VMEM(bins_shape, bf16),
+            pltpu.VMEM(q_short.shape, bf16),
+            pltpu.VMEM(q_long.shape, bf16),
+            dma((BINS + PIECES,)),
+            dma((BINS + PIECES,)),
+        ],
+        compiler_params=pltpu.CompilerParams(vmem_limit_bytes=56 * 2**20),
+    )(bins, long)
 
 
 def solution(mesh):

time: 53.7 us -> 50.5 us (0.940)
  the two profiles are of different devices: /device:TPU:2 before, /device:TPU:24 now
where the time goes in v3:
time: 50.5 us; the launch traced here: 50.3 us
  Pallas kernels  49.7 us (98%)
  between operations  0.64 us (1%)
    pallas_call x1, Pallas kernels, local(): pl.pallas_call(kernel, out_shape=[jax.ShapeDtypeStruct(bins_shape, bf16),...  47.4 us
    pallas_call x1, Pallas kernels, local(): pl.pallas_call(finish, out_shape=[jax.ShapeDtypeStruct(q_short.shape, bf1...  2.34 us

profile of v3, /device:TPU:24, one launch (start us, length us, event | category | flops | bytes accessed | tf_op | source)
XLA Modules:
  0.0 50.3 jit_solution(17872337510074830871)
XLA Ops:
  0.6 47.4 %shard_map.122 = (bf16[2,4,32,640]{3,2,1,0:T(8,128)(2,1)}, bf16[128,2048]{1,0:T(8,128)(2,1)}) custom-call(s32[65536]{0:T(1024)} %constant.4.clone.table_any, f32[1,128]{1,0:T(1,128)} %constant.5.clone.inverse_any, s32[1,3,2,64]{3,2,1,0:T(2,128)} %bitcast.2, s32[1,2,64]{2,1,0:T(2,128)} %bitcast.3, s32[1,3]{1,0:T(1,128)} %long_lengths_any.1, ...), custom_call_target="tpu_custom_call" | custom-call | tf_op jit(solution)/shard_map/pallas_call | solution.py:523
  48.0 2.3 %shard_map.123 = (bf16[128,2048]{1,0:T(8,128)(2,1)}, bf16[128,2048]{1,0:T(8,128)(2,1)}) custom-call(bf16[2,4,32,640]{3,2,1,0:T(8,128)(2,1)} %get-tuple-element.4.bins_any, bf16[128,2048]{1,0:T(8,128)(2,1)} %get-tuple-element.5.long_any), custom_call_target="tpu_custom_call" | custom-call | tf_op jit(solution)/shard_map/pallas_call | solution.py:558

commit v4 on v3

--- a/solution.py
+++ b/solution.py
@@ -322,10 +322,8 @@
 
     def ring(n):
         for way in range(2):
-            ring_copy(n, way).wait_recv()
-
-        @pl.when(n + KVHEADS < Y_SENDS)
-        def _():
+            ring_copy(n, way).wait()
+        if n + KVHEADS < Y_SENDS:
             for way in range(2):
                 ring_copy(n + KVHEADS, way).start()
 
@@ -377,48 +375,47 @@
     third = [3, HOPS + 3]
     far = [HOPS]
 
-    def one_step(step, work, rings=(True, True)):
+    plan = [
+        [(ring, 0), (prepare, 0)],
+        [(ring, 1), (prepare, 1)],
+        [(prepare, 2), (prepare, 3)],
+        [(ring, 2)],
+        [(ring, 3), (attend, [0], near)],
+        [(ring, 4), (attend, [1], near)],
+        [(ring, 5), (attend, [2], near)],
+        [(attend, [3], near)],
+        [(ring, 6)],
+        [(ring, 7), (attend, [0], middle)],
+        [(ring, 8), (attend, [1], middle)],
+        [(ring, 9), (attend, [2], middle)],
+        [(attend, [3], middle)],
+        [(ring, 10)],
+        [(ring, 11), (attend, [1], third)],
+        [(ring, 12), (attend, [3], third)],
+    ]
+    last = [[(attend, [0], third + far)], [(attend, [2], third + far)]]
+
+    def work(tasks):
+        for task, *arguments in tasks:
+            task(*arguments)
+
+    loads[10].wait()
+    for step in range(STEPS):
         for t in streams:
-            phase, half = 2 * step + t // HALVES, t % HALVES
-            if not (isinstance(step, int) and step == 0):
+            if step == 0:
+                mate_copy(t).wait()
+            else:
                 collect(t, step - 1)
             send(t, step)
-            if half == 0 and rings[t // HALVES]:
-                ring(phase - 1)
-            work(phase, [half] if HALVES > 1 else [0, 1])
-            if not (isinstance(step, int) and step == 0):
+            if t % HALVES == 0:
+                work(plan[2 * step + t // HALVES])
+            if step > 0:
                 all_of(len(streams) * (step - 1) + t).wait_send()
-
-    def preparing(phase, halves):
-        if 0 in halves:
-            prepare(phase)
-
-    def attending(pick, blocks):
-        def work(phase, halves):
-            if 0 in halves:
-                attend(pick(phase), blocks)
-
-        return work
-
-    loads[10].wait()
-    for t in streams:
-        mate_copy(t).wait()
-    one_step(0, preparing, (False, True))
-    one_step(1, preparing)
-
-    @pl.loop(2, 4)
-    def _(step):
-        one_step(step, attending(lambda p: [p - 4], near))
-
-    @pl.loop(4, 6)
-    def _(step):
-        one_step(step, attending(lambda p: [p - 8], middle))
-
-    one_step(6, attending(lambda p: {12: (0, 1), 13: (2, 3)}[p], third))
-    one_step(7, attending(lambda p: {14: (0, 2), 15: (1, 3)}[p], far), (True, False))
 
     for t in streams:
         collect(t, STEPS - 1)
+        if t % HALVES == 0:
+            work(last[t // HALVES])
 
     swap = (dp ^ masks[0]) > (dp ^ masks[1])
     for g in range(CHUNKS):
@@ -432,14 +429,11 @@
         bin_result[1, g] = jnp.where(swap, chunks[0], chunks[1])
         for m in range(BINS):
             bin_copy(m, g).start()
+    ring(Y_SENDS - 1)
+    attend([1, 3], far)
 
     for t in streams:
         all_of(len(streams) * (STEPS - 1) + t).wait_send()
-
-    @pl.loop(0, Y_SENDS)
-    def _(n):
-        for way in range(2):
-            ring_copy(n, way).wait_send()
 
     for g in range(CHUNKS):
         long_copy(g).wait()

time: 50.5 us -> 53.5 us (1.059)
  Pallas kernels: 49.7 us -> 52.6 us
    pallas_call x1, Pallas kernels: 47.4 us -> 50.3 us  [local(): pl.pallas_call(kernel, out_shape=[jax.ShapeDtypeStruct(bins_shape, bf16),...]
where the time goes in v4:
time: 53.5 us; the launch traced here: 53.2 us
  Pallas kernels  52.6 us (98%)
  between operations  0.64 us (1%)
    pallas_call x1, Pallas kernels, local(): pl.pallas_call(kernel, out_shape=[jax.ShapeDtypeStruct(bins_shape, bf16),...  50.3 us
    pallas_call x1, Pallas kernels, local(): pl.pallas_call(finish, out_shape=[jax.ShapeDtypeStruct(q_short.shape, bf1...  2.34 us

profile of v4, /device:TPU:24, one launch (start us, length us, event | category | flops | bytes accessed | tf_op | source)
XLA Modules:
  0.0 53.2 jit_solution(16561967946816847124)
XLA Ops:
  0.6 50.3 %shard_map.122 = (bf16[2,4,32,640]{3,2,1,0:T(8,128)(2,1)}, bf16[128,2048]{1,0:T(8,128)(2,1)}) custom-call(s32[65536]{0:T(1024)} %constant.4.clone.table_any, f32[1,128]{1,0:T(1,128)} %constant.5.clone.inverse_any, s32[1,3,2,64]{3,2,1,0:T(2,128)} %bitcast.2, s32[1,2,64]{2,1,0:T(2,128)} %bitcast.3, s32[1,3]{1,0:T(1,128)} %long_lengths_any.1, ...), custom_call_target="tpu_custom_call" | custom-call | tf_op jit(solution)/shard_map/pallas_call | solution.py:517
  50.9 2.3 %shard_map.123 = (bf16[128,2048]{1,0:T(8,128)(2,1)}, bf16[128,2048]{1,0:T(8,128)(2,1)}) custom-call(bf16[2,4,32,640]{3,2,1,0:T(8,128)(2,1)} %get-tuple-element.4.bins_any, bf16[128,2048]{1,0:T(8,128)(2,1)} %get-tuple-element.5.long_any), custom_call_target="tpu_custom_call" | custom-call | tf_op jit(solution)/shard_map/pallas_call | solution.py:552

commit v5 on v3

--- a/solution.py
+++ b/solution.py
@@ -22,9 +22,7 @@
 SCALE = math.log2(math.e) / math.sqrt(HEAD_DIM)
 
 NZ, NX, NY = 8, 4, 8
-HALVES = 1
 EARLY = BIN_LEN // 2
-ROWS = EARLY // HALVES
 CUTS = (0, HEAD_DIM, 2 * HEAD_DIM, 4 * HEAD_DIM, 5 * HEAD_DIM)
 CHUNKS = KVHEADS
 STEPS = 8
@@ -127,12 +125,12 @@
 
 
 def lanes_at(i, width):
-    return pl.ds(i * width, width)
+    return pl.ds(pl.multiple_of(i * width, width), width)
 
 
 def stacked_heads(q_ref, g, cosine, sine):
-    heads = range(g * GROUP, (g + 1) * GROUP)
-    return jnp.concatenate([rotated(q_ref[:, lanes(h, HEAD_DIM)], cosine, sine) for h in heads], 0)
+    parts = [q_ref[:, lanes_at(g * GROUP + i, HEAD_DIM)] for i in range(GROUP)]
+    return jnp.concatenate([rotated(part, cosine, sine) for part in parts], 0)
 
 
 def score(query, key):
@@ -152,7 +150,8 @@
     bin_out, long_out,
     table, dest, inverse, lengths, long_lengths,
     k_long, v_long, q_short, k_short, v_short, q_long,
-    pool_refs, stage, landing, kv, query, top, acc, bias_ref, bin_result, long_result,
+    pool, stage, landing, kv, query, top, acc, bias_ref, short_bias, short_turn, long_turn,
+    bin_result, long_result,
     load_sem, out_sem, mate_send, mate_recv, route_send, route_recv, y_send, y_recv,
 ):
     dp, ctx = lax.axis_index("dp"), lax.axis_index("ctx")
@@ -227,21 +226,25 @@
 
     for load in loads[5:7]:
         load.wait()
-    for g in range(KVHEADS):
-        kv[0, g, :, :HEAD_DIM] = rotated(k_long[:, lanes(g, HEAD_DIM)], long_cos, long_sin)
-        kv[0, g, :, HEAD_DIM:] = v_long[:, lanes(g, HEAD_DIM)]
+    short_turn[0], short_turn[1] = short_cos, short_sin
+    long_turn[0], long_turn[1] = long_cos, long_sin
+
+    @pl.loop(0, KVHEADS)
+    def _(g):
+        kv[0, g, :, :HEAD_DIM] = rotated(k_long[:, lanes_at(g, HEAD_DIM)], long_turn[0], long_turn[1])
+        kv[0, g, :, HEAD_DIM:] = v_long[:, lanes_at(g, HEAD_DIM)]
+
     pl.semaphore_wait(barrier, 3 + DIRS)
-    for n in range(KVHEADS):
+
+    @pl.loop(0, KVHEADS)
+    def _(n):
         for way in range(2):
             ring_copy(n, way).start()
 
-    pools = [*pool_refs]
-    streams = range(BINS * HALVES)
-
-    def mate_copy(t):
+    def mate_copy(j):
         return copy(
-            pools[t].at[pl.ds(0, CHUNKS)], pools[t].at[pl.ds(CHUNKS, CHUNKS)],
-            mate_send.at[t], mate_recv.at[t], mate,
+            pool.at[j, pl.ds(0, CHUNKS)], pool.at[j, pl.ds(CHUNKS, CHUNKS)],
+            mate_send.at[j], mate_recv.at[j], mate,
         )
 
     for load in loads[7:10]:
@@ -250,53 +253,50 @@
     def bias_of(rows, reach):
         index = lane[rows] % reach
         allowed = (index >= short_start[rows]) & (index <= token[rows])
-        return jnp.concatenate([jnp.where(allowed, 0.0, NEGATIVE)] * GROUP, 0)
+        return jnp.where(allowed, 0.0, NEGATIVE)
 
     spot = lane[:EARLY]
-    for j in range(BINS):
-        rows = slice(j * BIN_LEN, (j + 1) * BIN_LEN)
-        early = slice(j * BIN_LEN, j * BIN_LEN + EARLY)
-        late = slice(j * BIN_LEN + EARLY, (j + 1) * BIN_LEN)
-        early_bias, late_bias = bias_of(early, EARLY), bias_of(late, BIN_LEN)
-        early_scores, late_scores = [], []
-        for g in range(CHUNKS):
-            heads = [
-                rotated(q_short[rows, lanes(g * GROUP + i, HEAD_DIM)], short_cos[rows], short_sin[rows])
-                for i in range(GROUP)
-            ]
-            key = rotated(k_short[rows, lanes(g, HEAD_DIM)], short_cos[rows], short_sin[rows])
-            first = jnp.concatenate([q[:EARLY] for q in heads], 0)
-            second = jnp.concatenate([q[EARLY:] for q in heads], 0)
-            keys = jnp.concatenate([key[:EARLY]] * GROUP, 0)
-            early_scores.append(score(first, keys) + early_bias)
-            late_scores.append(score(second, jnp.concatenate([key] * 2, 0)) + late_bias)
-        scores = jnp.concatenate(early_scores + late_scores, 0)
+    spans = [slice(i * EARLY, (i + 1) * EARLY) for i in range(2 * BINS)]
+    for i, rows in enumerate(spans):
+        short_bias[i] = bias_of(rows, (EARLY, BIN_LEN)[i % 2])
+
+    @pl.loop(0, CHUNKS)
+    def _(g):
+        cosine, sine = short_turn[0], short_turn[1]
+        heads = [
+            rotated(q_short[:, lanes_at(g * GROUP + i, HEAD_DIM)], cosine, sine) for i in range(GROUP)
+        ]
+        key = rotated(k_short[:, lanes_at(g, HEAD_DIM)], cosine, sine)
+        values = v_short[:, lanes_at(g, HEAD_DIM)]
+        scores = []
+        for i, rows in enumerate(spans):
+            queries = jnp.concatenate([q[rows] for q in heads], 0)
+            if i % 2:
+                keys = jnp.concatenate([key[spans[i - 1]], key[rows]] * 2, 0)
+            else:
+                keys = jnp.concatenate([key[rows]] * GROUP, 0)
+            scores.append(score(queries, keys) + jnp.concatenate([short_bias[i]] * GROUP, 0))
+        scores = jnp.concatenate(scores, 0)
         weight = jnp.exp2(scores - jnp.max(scores, axis=1, keepdims=True))
-        for g in range(CHUNKS):
-            w = [weight[(g * GROUP + i) * EARLY :][:EARLY] for i in range(GROUP)]
+        for j in range(BINS):
+            w = [weight[(2 * j * GROUP + i) * EARLY :][:EARLY] for i in range(2 * GROUP)]
             packed = w[0]
             for i in range(1, GROUP):
                 packed = jnp.where(spot // EARLY == i, w[i], packed)
-            w = [weight[((CHUNKS + g) * GROUP + i) * EARLY :][:EARLY] for i in range(GROUP)]
-            left = jnp.where(spot < BIN_LEN, w[0], w[1])
-            right = jnp.where(spot < BIN_LEN, w[2], w[3])
-            pieces = [
-                packed.astype(jnp.bfloat16), v_short[early, lanes(g, HEAD_DIM)],
-                jnp.concatenate([left, right], 1).astype(jnp.bfloat16), v_short[late, lanes(g, HEAD_DIM)],
-            ]
-            for h in range(HALVES):
-                for i, piece in enumerate(pieces):
-                    part = slice(CUTS[i], CUTS[i + 1])
-                    pools[j * HALVES + h][g, :, part] = piece[h * ROWS : (h + 1) * ROWS]
-        for h in range(HALVES):
-            mate_copy(j * HALVES + h).start()
+            left = jnp.where(spot < BIN_LEN, w[GROUP], w[GROUP + 1])
+            right = jnp.where(spot < BIN_LEN, w[GROUP + 2], w[GROUP + 3])
+            pool[j, g, :, CUTS[0] : CUTS[1]] = packed.astype(jnp.bfloat16)
+            pool[j, g, :, CUTS[1] : CUTS[2]] = values[spans[2 * j]]
+            pool[j, g, :, CUTS[2] : CUTS[3]] = jnp.concatenate([left, right], 1).astype(jnp.bfloat16)
+            pool[j, g, :, CUTS[3] : CUTS[4]] = values[spans[2 * j + 1]]
+
+    for j in range(BINS):
+        mate_copy(j).start()
 
     for load in loads[:2]:
         load.wait()
-    masks = [dest[0, j, 0] for j in range(BINS)]
-
-    def entry(t, place):
-        mask = masks[t // HALVES]
+    def entry(j, place):
+        mask = dest[0, j, 0]
         index = table[(mask >> 1) * ROUTE + place]
         return index + jnp.where(index < CHUNKS, (mask & 1) * CHUNKS, 0)
 
@@ -308,16 +308,14 @@
     def all_of(slot):
         return copy(stage.at[slot], landing.at[slot], route_send.at[slot], route_recv.at[slot], routes[0])
 
-    def collect(t, step):
-        slot = len(streams) * step + t
+    def collect(slot):
         all_of(slot).wait_recv()
         for d in range(DIRS):
-            pools[t][OWN + DIRS * step + d] = landing[slot, d]
-
-    def send(t, step):
-        slot = len(streams) * step + t
+            pool[slot % BINS, OWN + DIRS * (slot // BINS) + d] = landing[slot, d]
+
+    def send(slot):
         for d in range(DIRS):
-            stage[slot, d] = pools[t][entry(t, step * DIRS + d)]
+            stage[slot, d] = pool[slot % BINS, entry(slot % BINS, slot // BINS * DIRS + d)]
             route_copy(slot, d).start()
 
     def ring(n):
@@ -329,119 +327,101 @@
             for way in range(2):
                 ring_copy(n + KVHEADS, way).start()
 
-    shift = [0] + [-h for h in range(1, HOPS + 1)] + [h for h in range(1, NY - HOPS)]
-
-    def prepare(t):
-        query[t] = stacked_heads(q_long, t, long_cos, long_sin)
-        for i in (2 * t, 2 * t + 1):
-            key_index = lane + (ctx + NY + shift[i]) % NY * span
+    loads[10].wait()
+
+    @pl.loop(0, KVHEADS)
+    def _(g):
+        query[g] = stacked_heads(q_long, g, long_turn[0], long_turn[1])
+        top[g] = jnp.full(top.shape[1:], NEGATIVE)
+        acc[g] = jnp.zeros(acc.shape[1:])
+        for i in (2 * g, 2 * g + 1):
+            shift = jnp.where(i <= HOPS, NY - i, i - HOPS)
+            key_index = lane + (ctx + shift) % NY * span
             allowed = (key_index >= long_start) & (key_index <= my_row)
             bias_ref[i] = jnp.where(allowed, 0.0, NEGATIVE)
 
-    def attend(heads, blocks):
-        begins, ends = 0 in blocks, HOPS in blocks
+    def attend(u):
+        turn = u // KVHEADS
+        g = jnp.where(turn == HOPS - 1, u % 2 * 2 + u // 2 % 2, u % KVHEADS)
+        blocks = [jnp.where(turn == 0, 0, turn + HOPS), turn + 1]
         bias = jnp.concatenate([bias_ref[i] for i in blocks], 1)
-        bias = jnp.concatenate([bias] * GROUP, 0)
-        keys = [jnp.concatenate([kv[i, g, :, :HEAD_DIM] for i in blocks], 0) for g in heads]
-        values = [jnp.concatenate([kv[i, g, :, HEAD_DIM:] for i in blocks], 0) for g in heads]
-        scores = [score(query[g], k) + bias for g, k in zip(heads, keys)]
-        peaks = [jnp.max(s, axis=1, keepdims=True) for s in scores]
-        if not begins:
-            olds = [top[g][:, :1] for g in heads]
-            peaks = [jnp.maximum(peak, old) for peak, old in zip(peaks, olds)]
-        weights = [jnp.exp2(s - peak) for s, peak in zip(scores, peaks)]
-        blended = [blend(w, v) for w, v in zip(weights, values)]
-        for n, g in enumerate(heads):
-            both = blended[n]
-            if not begins:
-                both = both + acc[g] * jnp.exp2(olds[n] - peaks[n])
-            if ends:
-                result = (both[:, :HEAD_DIM] / both[:, HEAD_DIM:]).astype(jnp.bfloat16)
-                for i in range(GROUP):
-                    long_result[:, lanes(g * GROUP + i, HEAD_DIM)] = result[i * span : (i + 1) * span]
-                long_copy(g).start()
-            else:
-                top[g] = jnp.broadcast_to(peaks[n], top.shape[1:])
-                acc[g] = both
+        keys = jnp.concatenate([kv[i, g, :, :HEAD_DIM] for i in blocks], 0)
+        values = jnp.concatenate([kv[i, g, :, HEAD_DIM:] for i in blocks], 0)
+        scores = score(query[g], keys) + jnp.concatenate([bias] * GROUP, 0)
+        old = top[g]
+        peak = jnp.maximum(jnp.max(scores, axis=1, keepdims=True), old[:, :1])
+        blended = blend(jnp.exp2(scores - peak), values)
+        acc[g] = blended + acc[g] * jnp.exp2(old[:, :1] - peak)
+        top[g] = jnp.broadcast_to(peak, old.shape)
 
     def long_copy(g):
+        part = lanes_at(g, WIDE)
         return pltpu.make_async_copy(
-            long_result.at[:, lanes_at(g, WIDE)], long_out.at[:, lanes_at(g, WIDE)], out_sem.at[BINS * CHUNKS + g]
+            long_result.at[:, part], long_out.at[:, part], out_sem.at[BINS * CHUNKS + g]
         )
 
     def bin_copy(m, g):
         return pltpu.make_async_copy(bin_result.at[m, g], bin_out.at[m, g], out_sem.at[m * CHUNKS + g])
 
-    near = [0, 1, HOPS + 1]
-    middle = [2, HOPS + 2]
-    third = [3, HOPS + 3]
-    far = [HOPS]
-
-    def one_step(step, work, rings=(True, True)):
-        for t in streams:
-            phase, half = 2 * step + t // HALVES, t % HALVES
-            if not (isinstance(step, int) and step == 0):
-                collect(t, step - 1)
-            send(t, step)
-            if half == 0 and rings[t // HALVES]:
-                ring(phase - 1)
-            work(phase, [half] if HALVES > 1 else [0, 1])
-            if not (isinstance(step, int) and step == 0):
-                all_of(len(streams) * (step - 1) + t).wait_send()
-
-    def preparing(phase, halves):
-        if 0 in halves:
-            prepare(phase)
-
-    def attending(pick, blocks):
-        def work(phase, halves):
-            if 0 in halves:
-                attend(pick(phase), blocks)
-
-        return work
-
-    loads[10].wait()
-    for t in streams:
-        mate_copy(t).wait()
-    one_step(0, preparing, (False, True))
-    one_step(1, preparing)
-
-    @pl.loop(2, 4)
-    def _(step):
-        one_step(step, attending(lambda p: [p - 4], near))
-
-    @pl.loop(4, 6)
-    def _(step):
-        one_step(step, attending(lambda p: [p - 8], middle))
-
-    one_step(6, attending(lambda p: {12: (0, 1), 13: (2, 3)}[p], third))
-    one_step(7, attending(lambda p: {14: (0, 2), 15: (1, 3)}[p], far), (True, False))
-
-    for t in streams:
-        collect(t, STEPS - 1)
-
-    swap = (dp ^ masks[0]) > (dp ^ masks[1])
-    for g in range(CHUNKS):
-        chunks = [
-            jnp.concatenate(
-                [pools[t][entry(t, DIRS * STEPS + g)] for t in range(j * HALVES, (j + 1) * HALVES)], 0
-            )
-            for j in range(BINS)
-        ]
+    slots = BINS * STEPS
+    for j in range(BINS):
+        mate_copy(j).wait()
+
+    @pl.loop(0, slots)
+    def _(slot):
+        @pl.when(slot >= BINS)
+        def _():
+            collect(slot - BINS)
+
+        send(slot)
+
+        @pl.when((slot >= 1) & (slot <= Y_SENDS))
+        def _():
+            ring(slot - 1)
+
+        full = (HOPS - 1) * KVHEADS
+        begin = jnp.where(slot <= full + 1, jnp.maximum(slot - 1, 0), jnp.minimum(2 * slot - 2 - full, 4 * HOPS))
+        end = jnp.where(slot <= full, slot, jnp.minimum(2 * slot - full, 4 * HOPS))
+
+        @pl.loop(begin, end)
+        def _(u):
+            attend(u)
+
+        @pl.when(slot >= BINS)
+        def _():
+            all_of(slot - BINS).wait_send()
+
+    @pl.loop(0, KVHEADS)
+    def _(g):
+        both = acc[g]
+        result = (both[:, :HEAD_DIM] / both[:, HEAD_DIM:]).astype(jnp.bfloat16)
+        for i in range(GROUP):
+            long_result[:, lanes_at(g * GROUP + i, HEAD_DIM)] = result[i * span : (i + 1) * span]
+        long_copy(g).start()
+
+    for slot in range(slots - BINS, slots):
+        collect(slot)
+
+    swap = (dp ^ dest[0, 0, 0]) > (dp ^ dest[0, 1, 0])
+
+    @pl.loop(0, CHUNKS)
+    def _(g):
+        chunks = [pool[j, entry(j, DIRS * STEPS + g)] for j in range(BINS)]
         bin_result[0, g] = jnp.where(swap, chunks[1], chunks[0])
         bin_result[1, g] = jnp.where(swap, chunks[0], chunks[1])
         for m in range(BINS):
             bin_copy(m, g).start()
 
-    for t in streams:
-        all_of(len(streams) * (STEPS - 1) + t).wait_send()
+    for slot in range(slots - BINS, slots):
+        all_of(slot).wait_send()
 
     @pl.loop(0, Y_SENDS)
     def _(n):
         for way in range(2):
             ring_copy(n, way).wait_send()
 
-    for g in range(CHUNKS):
+    @pl.loop(0, CHUNKS)
+    def _(g):
         long_copy(g).wait()
         for m in range(BINS):
             bin_copy(m, g).wait()
@@ -483,23 +463,26 @@
 
     for m in range(BINS):
         pieces[m][0].wait()
-        for g in range(CHUNKS):
-            chunk = bins[m, g]
-            first, first_v, second, second_v = [chunk[:, CUTS[i] : CUTS[i + 1]] for i in range(4)]
-            early = jnp.concatenate([first * q for q in quarter], 0)
-            late = [second[:, lanes(i // 2, HEAD_DIM)] * side[i % 2] for i in range(GROUP)]
-            late = jnp.concatenate(late, 0)
-            start = m * BIN_LEN
-            short[start : start + EARLY, lanes(g, WIDE)] = finished(
-                early, jnp.concatenate([first_v] * GROUP, 0)
-            )
-            short[start + EARLY : start + BIN_LEN, lanes(g, WIDE)] = finished(
-                late, jnp.concatenate([first_v, second_v] * 2, 0)
-            )
-        if m == 0:
-            for load, store in pieces[BINS:]:
-                load.wait()
-                store.start()
+
+    @pl.loop(0, BINS * CHUNKS)
+    def _(n):
+        m, g = n // CHUNKS, n % CHUNKS
+        first, first_v, second, second_v = [bins[m, g, :, CUTS[i] : CUTS[i + 1]] for i in range(4)]
+        early = jnp.concatenate([first * q for q in quarter], 0)
+        late = [second[:, lanes(i // 2, HEAD_DIM)] * side[i % 2] for i in range(GROUP)]
+        late = jnp.concatenate(late, 0)
+        parts = [
+            finished(early, jnp.concatenate([first_v] * GROUP, 0)),
+            finished(late, jnp.concatenate([first_v, second_v] * 2, 0)),
+        ]
+        for i, part in enumerate(parts):
+            rows = pl.ds(pl.multiple_of(m * BIN_LEN + i * EARLY, EARLY), EARLY)
+            short[rows, lanes_at(g, WIDE)] = part
+
+    for load, store in pieces[BINS:]:
+        load.wait()
+        store.start()
+    for m in range(BINS):
         pieces[m][1].start()
     for _, store in pieces:
         store.wait()
@@ -516,7 +499,7 @@
     dest = jnp.transpose(bin_dest, (1, 2, 0))
 
     bf16, f32, i32 = jnp.bfloat16, jnp.float32, jnp.int32
-    slots = BINS * HALVES * STEPS
+    slots = BINS * STEPS
     dma = pltpu.SemaphoreType.DMA
     inputs = [k_long, v_long, q_short, k_short, v_short, q_long]
     bins_shape = (BINS, CHUNKS, EARLY, CUTS[-1])
@@ -532,20 +515,23 @@
             pltpu.VMEM(lengths.shape, i32),
             pltpu.VMEM(long_lengths.shape, i32),
             *[pltpu.VMEM(a.shape, bf16) for a in inputs],
-            [pltpu.VMEM((POOL, ROWS, CUTS[-1]), bf16)] * (BINS * HALVES),
-            pltpu.VMEM((slots, DIRS, ROWS, CUTS[-1]), bf16),
-            pltpu.VMEM((slots, DIRS, ROWS, CUTS[-1]), bf16),
+            pltpu.VMEM((BINS, POOL, EARLY, CUTS[-1]), bf16),
+            pltpu.VMEM((slots, DIRS, EARLY, CUTS[-1]), bf16),
+            pltpu.VMEM((slots, DIRS, EARLY, CUTS[-1]), bf16),
             pltpu.VMEM((NY, KVHEADS, span, 2 * HEAD_DIM), bf16),
             pltpu.VMEM((KVHEADS, GROUP * span, HEAD_DIM), bf16),
             pltpu.VMEM((KVHEADS, GROUP * span, HEAD_DIM), f32),
             pltpu.VMEM((KVHEADS, GROUP * span, 2 * HEAD_DIM), f32),
             pltpu.VMEM((NY, span, span), f32),
+            pltpu.VMEM((2 * BINS, EARLY, HEAD_DIM), f32),
+            pltpu.VMEM((2, span, HEAD_DIM), f32),
+            pltpu.VMEM((2, span, HEAD_DIM), f32),
             pltpu.VMEM(bins_shape, bf16),
             pltpu.VMEM(q_long.shape, bf16),
             dma((11,)),
             dma((BINS * CHUNKS + KVHEADS,)),
-            dma((BINS * HALVES,)),
-            dma((BINS * HALVES,)),
+            dma((BINS,)),
+            dma((BINS,)),
             dma((slots,)),
             dma((slots,)),
             dma((2, Y_SENDS)),

time: 50.5 us -> 54.2 us (1.073)
  Pallas kernels: 49.7 us -> 53.4 us
    pallas_call x1, Pallas kernels: 47.4 us -> 49.9 us  [local(): pl.pallas_call(kernel, out_shape=[jax.ShapeDtypeStruct(bins_shape, bf16),...]
    pallas_call x1, Pallas kernels: 2.34 us -> 3.54 us  [local(): pl.pallas_call(finish, out_shape=[jax.ShapeDtypeStruct(q_short.shape, bf1...]
where the time goes in v5:
time: 54.2 us; the launch traced here: 54.1 us
  Pallas kernels  53.4 us (99%)
  between operations  0.64 us (1%)
    pallas_call x1, Pallas kernels, local(): pl.pallas_call(kernel, out_shape=[jax.ShapeDtypeStruct(bins_shape, bf16),...  49.9 us
    pallas_call x1, Pallas kernels, local(): pl.pallas_call(finish, out_shape=[jax.ShapeDtypeStruct(q_short.shape, bf1...  3.54 us

profile of v5, /device:TPU:24, one launch (start us, length us, event | category | flops | bytes accessed | tf_op | source)
XLA Modules:
  0.0 54.1 jit_solution(7116317652520117966)
XLA Ops:
  0.6 49.9 %shard_map.122 = (bf16[2,4,32,640]{3,2,1,0:T(8,128)(2,1)}, bf16[128,2048]{1,0:T(8,128)(2,1)}) custom-call(s32[65536]{0:T(1024)} %constant.4.clone.table_any, f32[1,128]{1,0:T(1,128)} %constant.5.clone.inverse_any, s32[1,3,2,64]{3,2,1,0:T(2,128)} %bitcast.2, s32[1,2,64]{2,1,0:T(2,128)} %bitcast.3, s32[1,3]{1,0:T(1,128)} %long_lengths_any.1, ...), custom_call_target="tpu_custom_call" | custom-call | tf_op jit(solution)/shard_map/pallas_call | solution.py:506
  50.5 3.5 %shard_map.123 = (bf16[128,2048]{1,0:T(8,128)(2,1)}, bf16[128,2048]{1,0:T(8,128)(2,1)}) custom-call(bf16[2,4,32,640]{3,2,1,0:T(8,128)(2,1)} %get-tuple-element.4.bins_any, bf16[128,2048]{1,0:T(8,128)(2,1)} %get-tuple-element.5.long_any), custom_call_target="tpu_custom_call" | custom-call | tf_op jit(solution)/shard_map/pallas_call | solution.py:544

commit v6 on v4

--- a/solution.py
+++ b/solution.py
@@ -314,10 +314,10 @@
         for d in range(DIRS):
             pools[t][OWN + DIRS * step + d] = landing[slot, d]
 
-    def send(t, step):
+    def send(t, step, entries):
         slot = len(streams) * step + t
         for d in range(DIRS):
-            stage[slot, d] = pools[t][entry(t, step * DIRS + d)]
+            stage[slot, d] = pools[t][entries[d]]
             route_copy(slot, d).start()
 
     def ring(n):
@@ -376,24 +376,23 @@
     far = [HOPS]
 
     plan = [
-        [(ring, 0), (prepare, 0)],
-        [(ring, 1), (prepare, 1)],
-        [(prepare, 2), (prepare, 3)],
-        [(ring, 2)],
-        [(ring, 3), (attend, [0], near)],
-        [(ring, 4), (attend, [1], near)],
-        [(ring, 5), (attend, [2], near)],
-        [(attend, [3], near)],
+        [(prepare, 0)],
+        [(ring, 0), (prepare, 1)],
+        [(ring, 1), (prepare, 2)],
+        [(ring, 2), (prepare, 3)],
+        [(ring, 3), (attend, [0, 1], near)],
+        [(ring, 4)],
+        [(ring, 5), (attend, [2, 3], near)],
         [(ring, 6)],
-        [(ring, 7), (attend, [0], middle)],
-        [(ring, 8), (attend, [1], middle)],
-        [(ring, 9), (attend, [2], middle)],
-        [(attend, [3], middle)],
-        [(ring, 10)],
-        [(ring, 11), (attend, [1], third)],
-        [(ring, 12), (attend, [3], third)],
+        [(ring, 7)],
+        [(ring, 8), (attend, [0, 1], middle)],
+        [(ring, 9)],
+        [(ring, 10), (attend, [2, 3], middle)],
+        [(ring, 11)],
+        [(ring, 12)],
+        [(attend, [0, 2], third + far)],
+        [(ring, 13), (attend, [1, 3], third + far)],
     ]
-    last = [[(attend, [0], third + far)], [(attend, [2], third + far)]]
 
     def work(tasks):
         for task, *arguments in tasks:
@@ -402,11 +401,12 @@
     loads[10].wait()
     for step in range(STEPS):
         for t in streams:
+            entries = [entry(t, step * DIRS + d) for d in range(DIRS)]
             if step == 0:
                 mate_copy(t).wait()
             else:
                 collect(t, step - 1)
-            send(t, step)
+            send(t, step, entries)
             if t % HALVES == 0:
                 work(plan[2 * step + t // HALVES])
             if step > 0:
@@ -414,8 +414,6 @@
 
     for t in streams:
         collect(t, STEPS - 1)
-        if t % HALVES == 0:
-            work(last[t // HALVES])
 
     swap = (dp ^ masks[0]) > (dp ^ masks[1])
     for g in range(CHUNKS):
@@ -429,9 +427,6 @@
         bin_result[1, g] = jnp.where(swap, chunks[0], chunks[1])
         for m in range(BINS):
             bin_copy(m, g).start()
-    ring(Y_SENDS - 1)
-    attend([1, 3], far)
-
     for t in streams:
         all_of(len(streams) * (STEPS - 1) + t).wait_send()
 

time: 53.5 us -> 50.3 us (0.940)
  Pallas kernels: 52.6 us -> 49.5 us
    pallas_call x1, Pallas kernels: 50.3 us -> 47.1 us  [local(): pl.pallas_call(kernel, out_shape=[jax.ShapeDtypeStruct(bins_shape, bf16),...]
where the time goes in v6:
time: 50.3 us; the launch traced here: 50.1 us
  Pallas kernels  49.5 us (98%)
  between operations  0.64 us (1%)
    pallas_call x1, Pallas kernels, local(): pl.pallas_call(kernel, out_shape=[jax.ShapeDtypeStruct(bins_shape, bf16),...  47.1 us
    pallas_call x1, Pallas kernels, local(): pl.pallas_call(finish, out_shape=[jax.ShapeDtypeStruct(q_short.shape, bf1...  2.34 us

profile of v6, /device:TPU:24, one launch (start us, length us, event | category | flops | bytes accessed | tf_op | source)
XLA Modules:
  0.0 50.1 jit_solution(1624827217445393167)
XLA Ops:
  0.6 47.1 %shard_map.122 = (bf16[2,4,32,640]{3,2,1,0:T(8,128)(2,1)}, bf16[128,2048]{1,0:T(8,128)(2,1)}) custom-call(s32[65536]{0:T(1024)} %constant.4.clone.table_any, f32[1,128]{1,0:T(1,128)} %constant.5.clone.inverse_any, s32[1,3,2,64]{3,2,1,0:T(2,128)} %bitcast.2, s32[1,2,64]{2,1,0:T(2,128)} %bitcast.3, s32[1,3]{1,0:T(1,128)} %long_lengths_any.1, ...), custom_call_target="tpu_custom_call" | custom-call | tf_op jit(solution)/shard_map/pallas_call | solution.py:512
  47.8 2.3 %shard_map.123 = (bf16[128,2048]{1,0:T(8,128)(2,1)}, bf16[128,2048]{1,0:T(8,128)(2,1)}) custom-call(bf16[2,4,32,640]{3,2,1,0:T(8,128)(2,1)} %get-tuple-element.4.bins_any, bf16[128,2048]{1,0:T(8,128)(2,1)} %get-tuple-element.5.long_any), custom_call_target="tpu_custom_call" | custom-call | tf_op jit(solution)/shard_map/pallas_call | solution.py:547

commit v7 on v6

--- a/solution.py
+++ b/solution.py
@@ -29,7 +29,7 @@
 CHUNKS = KVHEADS
 STEPS = 8
 DIRS = 4
-OWN = 2 * CHUNKS
+OWN = CHUNKS
 POOL = OWN + DIRS * STEPS
 PIECES = 4
 ROUTE = 64
@@ -153,7 +153,7 @@
     table, dest, inverse, lengths, long_lengths,
     k_long, v_long, q_short, k_short, v_short, q_long,
     pool_refs, stage, landing, kv, query, top, acc, bias_ref, bin_result, long_result,
-    load_sem, out_sem, mate_send, mate_recv, route_send, route_recv, y_send, y_recv,
+    load_sem, out_sem, route_send, route_recv, y_send, y_recv,
 ):
     dp, ctx = lax.axis_index("dp"), lax.axis_index("ctx")
     core, x, z = dp % 2, (dp // 2) % NX, dp // (2 * NX)
@@ -179,12 +179,11 @@
     def at(z_to, x_to):
         return (((z_to + NZ) % NZ * NX + (x_to + NX) % NX) * 2 + core, ctx)
 
-    mate = (dp + 1 - 2 * core, ctx)
     routes = [at(z, x + 1), at(z, x - 1), at(z + 1, x), at(z - 1, x)]
     rings = [(dp, (ctx + 1) % NY), (dp, (ctx + NY - 1) % NY)]
 
     barrier = pltpu.get_barrier_semaphore()
-    for other in [mate, *routes, *rings]:
+    for other in [*routes, *rings]:
         pl.semaphore_signal(barrier, inc=1, device_id=other, device_id_type=MESH)
 
     def copy(source, target, send, recv, other):
@@ -230,19 +229,13 @@
     for g in range(KVHEADS):
         kv[0, g, :, :HEAD_DIM] = rotated(k_long[:, lanes(g, HEAD_DIM)], long_cos, long_sin)
         kv[0, g, :, HEAD_DIM:] = v_long[:, lanes(g, HEAD_DIM)]
-    pl.semaphore_wait(barrier, 3 + DIRS)
+    pl.semaphore_wait(barrier, 2 + DIRS)
     for n in range(KVHEADS):
         for way in range(2):
             ring_copy(n, way).start()
 
     pools = [*pool_refs]
     streams = range(BINS * HALVES)
-
-    def mate_copy(t):
-        return copy(
-            pools[t].at[pl.ds(0, CHUNKS)], pools[t].at[pl.ds(CHUNKS, CHUNKS)],
-            mate_send.at[t], mate_recv.at[t], mate,
-        )
 
     for load in loads[7:10]:
         load.wait()
@@ -288,17 +281,12 @@
                 for i, piece in enumerate(pieces):
                     part = slice(CUTS[i], CUTS[i + 1])
                     pools[j * HALVES + h][g, :, part] = piece[h * ROWS : (h + 1) * ROWS]
-        for h in range(HALVES):
-            mate_copy(j * HALVES + h).start()
-
     for load in loads[:2]:
         load.wait()
     masks = [dest[0, j, 0] for j in range(BINS)]
 
     def entry(t, place):
-        mask = masks[t // HALVES]
-        index = table[(mask >> 1) * ROUTE + place]
-        return index + jnp.where(index < CHUNKS, (mask & 1) * CHUNKS, 0)
+        return table[(masks[t // HALVES] >> 1) * ROUTE + place]
 
     def route_copy(slot, d):
         return copy(
@@ -402,9 +390,7 @@
     for step in range(STEPS):
         for t in streams:
             entries = [entry(t, step * DIRS + d) for d in range(DIRS)]
-            if step == 0:
-                mate_copy(t).wait()
-            else:
+            if step > 0:
                 collect(t, step - 1)
             send(t, step, entries)
             if t % HALVES == 0:
@@ -415,18 +401,13 @@
     for t in streams:
         collect(t, STEPS - 1)
 
-    swap = (dp ^ masks[0]) > (dp ^ masks[1])
-    for g in range(CHUNKS):
-        chunks = [
-            jnp.concatenate(
+    for j in range(BINS):
+        for g in range(CHUNKS):
+            bin_result[j, g] = jnp.concatenate(
                 [pools[t][entry(t, DIRS * STEPS + g)] for t in range(j * HALVES, (j + 1) * HALVES)], 0
             )
-            for j in range(BINS)
-        ]
-        bin_result[0, g] = jnp.where(swap, chunks[1], chunks[0])
-        bin_result[1, g] = jnp.where(swap, chunks[0], chunks[1])
-        for m in range(BINS):
-            bin_copy(m, g).start()
+            bin_copy(j, g).start()
+
     for t in streams:
         all_of(len(streams) * (STEPS - 1) + t).wait_send()
 
@@ -436,26 +417,31 @@
             bin_copy(m, g).wait()
 
 
-def finish(bins_any, long_any, out_short, out_long, bins, short, long, sem_in, sem_out):
+def hand_over(long_any, out_long, long, sem_in, sem_out):
     rows = long.shape[0] // PIECES
-
-    def long_copies(p):
+    pieces = []
+    for p in range(PIECES):
         part = pl.ds(p * rows, rows)
-        return (
-            pltpu.make_async_copy(long_any.at[part], long.at[part], sem_in.at[BINS + p]),
-            pltpu.make_async_copy(long.at[part], out_long.at[part], sem_out.at[BINS + p]),
-        )
-
-    def short_copies(m):
+        load = pltpu.make_async_copy(long_any.at[part], long.at[part], sem_in.at[p])
+        load.start()
+        pieces.append((load, pltpu.make_async_copy(long.at[part], out_long.at[part], sem_out.at[p])))
+    for load, store in pieces:
+        load.wait()
+        store.start()
+    for _, store in pieces:
+        store.wait()
+
+
+def finish(dest_any, bins_any, mate_any, out_short, dest, bins, short, dest_sem, sem_in, sem_out):
+    pieces = []
+    for m in range(BINS):
         part = pl.ds(m * BIN_LEN, BIN_LEN)
-        return (
-            pltpu.make_async_copy(bins_any.at[m], bins.at[m], sem_in.at[m]),
-            pltpu.make_async_copy(short.at[part], out_short.at[part], sem_out.at[m]),
-        )
-
-    pieces = [short_copies(m) for m in range(BINS)] + [long_copies(p) for p in range(PIECES)]
-    for load, _ in pieces:
+        load = pltpu.make_async_copy((bins_any, mate_any)[m], bins.at[m], sem_in.at[m])
         load.start()
+        pieces.append((load, pltpu.make_async_copy(short.at[part], out_short.at[part], sem_out.at[m])))
+
+    dest_copy = pltpu.make_async_copy(dest_any, dest, dest_sem)
+    dest_copy.start()
 
     spot = lax.broadcasted_iota(jnp.int32, (EARLY, HEAD_DIM), 1)
 
@@ -470,10 +456,17 @@
         result = (blended[:, :HEAD_DIM] / blended[:, HEAD_DIM:]).astype(jnp.bfloat16)
         return jnp.concatenate([result[i * EARLY : (i + 1) * EARLY] for i in range(GROUP)], 1)
 
+    dest_copy.wait()
+    for m in range(2):
+        pieces[m][0].wait()
+    dp = lax.axis_index("dp")
+    masks = [dest[0, j, 0] for j in range(BINS)]
+    swap = jnp.where((dp ^ masks[0]) > (dp ^ masks[1]), 1, 0)
     for m in range(BINS):
-        pieces[m][0].wait()
+        j = m ^ swap
+        crossed = jnp.where(j == 0, masks[0], masks[1]) & 1
         for g in range(CHUNKS):
-            chunk = bins[m, g]
+            chunk = bins[crossed, j, g]
             first, first_v, second, second_v = [chunk[:, CUTS[i] : CUTS[i + 1]] for i in range(4)]
             early = jnp.concatenate([first * q for q in quarter], 0)
             late = [second[:, lanes(i // 2, HEAD_DIM)] * side[i % 2] for i in range(GROUP)]
@@ -485,16 +478,13 @@
             short[start + EARLY : start + BIN_LEN, lanes(g, WIDE)] = finished(
                 late, jnp.concatenate([first_v, second_v] * 2, 0)
             )
-        if m == 0:
-            for load, store in pieces[BINS:]:
-                load.wait()
-                store.start()
         pieces[m][1].start()
     for _, store in pieces:
         store.wait()
 
 
 HBM = pl.BlockSpec(memory_space=pltpu.HBM)
+ANY = pl.BlockSpec(memory_space=pl.ANY)
 
 
 def local(q_short, k_short, v_short, short_lengths, bin_dest, q_long, k_long, v_long, long_lengths):
@@ -533,8 +523,6 @@
             pltpu.VMEM(q_long.shape, bf16),
             dma((11,)),
             dma((BINS * CHUNKS + KVHEADS,)),
-            dma((BINS * HALVES,)),
-            dma((BINS * HALVES,)),
             dma((slots,)),
             dma((slots,)),
             dma((2, Y_SENDS)),
@@ -544,20 +532,32 @@
             collective_id=0, has_side_effects=True, vmem_limit_bytes=56 * 2**20
         ),
     )(table, inverse, lengths, dest, long_lengths, *inputs)
-    return pl.pallas_call(
+    mate_bins = lax.ppermute(bins, "dp", [(i, i ^ 1) for i in range(lax.axis_size("dp"))])
+    out_long = pl.pallas_call(
+        hand_over,
+        out_shape=jax.ShapeDtypeStruct(q_long.shape, bf16),
+        in_specs=[ANY],
+        out_specs=HBM,
+        scratch_shapes=[pltpu.VMEM(q_long.shape, bf16), dma((PIECES,)), dma((PIECES,))],
+        compiler_params=pltpu.CompilerParams(vmem_limit_bytes=56 * 2**20),
+        cost_estimate=pl.CostEstimate(flops=0, bytes_accessed=4 * q_long.size, transcendentals=0),
+    )(long)
+    out_short = pl.pallas_call(
         finish,
-        out_shape=[jax.ShapeDtypeStruct(q_short.shape, bf16), jax.ShapeDtypeStruct(q_long.shape, bf16)],
-        in_specs=[HBM, HBM],
-        out_specs=[HBM, HBM],
+        out_shape=jax.ShapeDtypeStruct(q_short.shape, bf16),
+        in_specs=[ANY] * 3,
+        out_specs=HBM,
         scratch_shapes=[
-            pltpu.VMEM(bins_shape, bf16),
+            pltpu.SMEM(dest.shape, i32),
+            pltpu.VMEM((2, *bins_shape), bf16),
             pltpu.VMEM(q_short.shape, bf16),
-            pltpu.VMEM(q_long.shape, bf16),
-            dma((BINS + PIECES,)),
-            dma((BINS + PIECES,)),
+            dma,
+            dma((2,)),
+            dma((BINS,)),
         ],
-        compiler_params=pltpu.CompilerParams(vmem_limit_bytes=56 * 2**20),
-    )(bins, long)
+        compiler_params=pltpu.CompilerParams(vmem_limit_bytes=24 * 2**20),
+    )(dest, bins, mate_bins)
+    return (out_short, out_long)
 
 
 def solution(mesh):

time: 50.3 us -> 55 us (1.093)
  the two profiles are of different devices: /device:TPU:24 before, /device:TPU:1 now
where the time goes in v7:
time: 55 us; the launch traced here: 54.8 us
  Pallas kernels  46.2 us (84%)
  starting transfers between devices  7.89 us (14%)
  between operations  0.7 us (1%)
    pallas_call x1, Pallas kernels, local(): pl.pallas_call(kernel, out_shape=[jax.ShapeDtypeStruct(bins_shape, bf16),...  42.4 us
    ppermute x1, starting transfers between devices, local(): lax.ppermute(bins, 'dp', [(i, i ^ 1) for i in range(lax.axis_size('dp'))])  7.89 us
    pallas_call x1, Pallas kernels, local(): pl.pallas_call(finish, out_shape=jax.ShapeDtypeStruct(q_short.shape, bf16...  1.95 us
    pallas_call x1, Pallas kernels, local(): pl.pallas_call(hand_over, out_shape=jax.ShapeDtypeStruct(q_long.shape, bf...  1.86 us
  transfers between devices with their start and end apart: 1, of which 0 were waited for; matrix products, arithmetic and copies ran while one was open for 0% of the time, Pallas kernels for 3%

profile of v7, /device:TPU:1, one launch (start us, length us, event | category | flops | bytes accessed | tf_op | source)
XLA Modules:
  0.0 54.8 jit_solution(7451974045712899318)
XLA Ops:
  0.6 42.4 %shard_map.122 = (bf16[2,4,32,640]{3,2,1,0:T(8,128)(2,1)}, bf16[128,2048]{1,0:T(8,128)(2,1)}) custom-call(s32[65536]{0:T(1024)} %constant.4.clone.table_any, f32[1,128]{1,0:T(1,128)} %constant.5.clone.inverse_any, s32[1,3,2,64]{3,2,1,0:T(2,128)} %bitcast.4, s32[1,2,64]{2,1,0:T(2,128)} %bitcast.2, s32[1,3]{1,0:T(1,128)} %long_lengths_any.1, ...), custom_call_target="tpu_custom_call" | custom-call | tf_op jit(solution)/shard_map/pallas_call | solution.py:502
  43.0 7.9 %collective-permute-start = (bf16[2,4,32,640]{3,2,1,0:T(8,128)(2,1)}, bf16[2,4,32,640]{3,2,1,0:T(8,128)(2,1)S(1)}, u32[]{:S(2)}, u32[]{:S(2)}) collective-permute-start(bf16[2,4,32,640]{3,2,1,0:T(8,128)(2,1)} %get-tuple-element.4.bins_any), channel_id=1, source_target_pairs={{0,8},{8,0},{16,24},{24,16},{32,40},{40,32},{48,56},{56,48},{64,72... | collective-permute-start | bytes 983048 | tf_op jit(solution)/shard_map/ppermute | solution.py:535
  50.9 0.0 copy-start
  51.0 0.0 copy-start.1
  51.0 1.9 %shard_map.124 = bf16[128,2048]{1,0:T(8,128)(2,1)} custom-call(bf16[128,2048]{1,0:T(8,128)(2,1)} %get-tuple-element.5.long_any), custom_call_target="tpu_custom_call" | custom-call | bytes 1048576 | tf_op jit(solution)/shard_map/pallas_call | solution.py:536
  52.8 0.0 collective-permute-done.mate_any
  52.8 0.0 copy-done
  52.9 0.0 copy-done.1
  52.9 1.9 %shard_map.123 = bf16[128,2048]{1,0:T(8,128)(2,1)} custom-call(s32[1,2,64]{2,1,0:T(2,128)S(1)} %bitcast.3, bf16[2,4,32,640]{3,2,1,0:T(8,128)(2,1)S(1)} %copy-done, bf16[2,4,32,640]{3,2,1,0:T(8,128)(2,1)S(1)} %collective-permute-done.mate_any), custom_call_target="tpu_custom_call" | custom-call | tf_op jit(solution)/shard_map/pallas_call | solution.py:545
Async XLA Ops:
  43.0 9.8 %collective-permute-start = (bf16[2,4,32,640]{3,2,1,0:T(8,128)(2,1)}, bf16[2,4,32,640]{3,2,1,0:T(8,128)(2,1)S(1)}, u32[]{:S(2)}, u32[]{:S(2)}) collective-permute-start(bf16[2,4,32,640]{3,2,1,0:T(8,128)(2,1)} %get-tuple-element.4.bins_any), channel_id=1, source_target_pairs={{0,8},{8,0},{16,24},{24,16},{32,40},{40,32},{48,56},{56,48},{64,72... | collective-permute-start | bytes 983048 | tf_op jit(solution)/shard_map/ppermute | solution.py:535
  50.9 1.9 %copy-start = (bf16[2,4,32,640]{3,2,1,0:T(8,128)(2,1)S(1)}, bf16[2,4,32,640]{3,2,1,0:T(8,128)(2,1)}, u32[]{:S(2)}) copy-start(bf16[2,4,32,640]{3,2,1,0:T(8,128)(2,1)} %get-tuple-element.4.bins_any) | copy-start | bytes 983044
  51.0 1.9 %copy-start.1 = (s32[64,1,2]{0,2,1:T(2,128)S(1)}, s32[64,1,2]{0,2,1:T(2,128)}, u32[]{:S(2)}) copy-start(s32[64,1,2]{0,2,1:T(2,128)} %param.15) | copy-start | bytes 1540

commit v8 on v6

--- a/solution.py
+++ b/solution.py
@@ -22,7 +22,7 @@
 SCALE = math.log2(math.e) / math.sqrt(HEAD_DIM)
 
 NZ, NX, NY = 8, 4, 8
-HALVES = 1
+HALVES = 2
 EARLY = BIN_LEN // 2
 ROWS = EARLY // HALVES
 CUTS = (0, HEAD_DIM, 2 * HEAD_DIM, 4 * HEAD_DIM, 5 * HEAD_DIM)
@@ -375,24 +375,10 @@
     third = [3, HOPS + 3]
     far = [HOPS]
 
-    plan = [
-        [(prepare, 0)],
-        [(ring, 0), (prepare, 1)],
-        [(ring, 1), (prepare, 2)],
-        [(ring, 2), (prepare, 3)],
-        [(ring, 3), (attend, [0, 1], near)],
-        [(ring, 4)],
-        [(ring, 5), (attend, [2, 3], near)],
-        [(ring, 6)],
-        [(ring, 7)],
-        [(ring, 8), (attend, [0, 1], middle)],
-        [(ring, 9)],
-        [(ring, 10), (attend, [2, 3], middle)],
-        [(ring, 11)],
-        [(ring, 12)],
-        [(attend, [0, 2], third + far)],
-        [(ring, 13), (attend, [1, 3], third + far)],
-    ]
+    nearer, rest = [near, middle], third + far
+    plan = [[(prepare, 0)], [(prepare, 1)], [(prepare, 2)], [(prepare, 3)]]
+    plan += [[(attend, [g], blocks)] for blocks in nearer for g in range(KVHEADS)]
+    plan += [[], [(attend, [0], rest)], [(attend, [2], rest)], [(attend, [1], rest)]]
 
     def work(tasks):
         for task, *arguments in tasks:
@@ -407,11 +393,15 @@
             else:
                 collect(t, step - 1)
             send(t, step, entries)
-            if t % HALVES == 0:
-                work(plan[2 * step + t // HALVES])
+            phase = 2 * step + t // HALVES
+            if t % HALVES == 0 and 0 < phase <= Y_SENDS:
+                ring(phase - 1)
+            if t % HALVES == HALVES - 1:
+                work(plan[phase])
             if step > 0:
                 all_of(len(streams) * (step - 1) + t).wait_send()
 
+    attend([3], rest)
     for t in streams:
         collect(t, STEPS - 1)
 

time: 50.3 us -> 49.5 us (0.984)
  the two profiles are of different devices: /device:TPU:24 before, /device:TPU:16 now
where the time goes in v8:
time: 49.5 us; the launch traced here: 49.3 us
  Pallas kernels  48.7 us (98%)
  between operations  0.64 us (1%)
    pallas_call x1, Pallas kernels, local(): pl.pallas_call(kernel, out_shape=[jax.ShapeDtypeStruct(bins_shape, bf16),...  46.3 us
    pallas_call x1, Pallas kernels, local(): pl.pallas_call(finish, out_shape=[jax.ShapeDtypeStruct(q_short.shape, bf1...  2.34 us

profile of v8, /device:TPU:16, one launch (start us, length us, event | category | flops | bytes accessed | tf_op | source)
XLA Modules:
  0.0 49.3 jit_solution(4161855317582011019)
XLA Ops:
  0.6 46.3 %shard_map.122 = (bf16[2,4,32,640]{3,2,1,0:T(8,128)(2,1)}, bf16[128,2048]{1,0:T(8,128)(2,1)}) custom-call(s32[65536]{0:T(1024)} %constant.4.clone.table_any, f32[1,128]{1,0:T(1,128)} %constant.5.clone.inverse_any, s32[1,3,2,64]{3,2,1,0:T(2,128)} %bitcast.2, s32[1,2,64]{2,1,0:T(2,128)} %bitcast.3, s32[1,3]{1,0:T(1,128)} %long_lengths_any.1, ...), custom_call_target="tpu_custom_call" | custom-call | tf_op jit(solution)/shard_map/pallas_call | solution.py:502
  47.0 2.3 %shard_map.123 = (bf16[128,2048]{1,0:T(8,128)(2,1)}, bf16[128,2048]{1,0:T(8,128)(2,1)}) custom-call(bf16[2,4,32,640]{3,2,1,0:T(8,128)(2,1)} %get-tuple-element.4.bins_any, bf16[128,2048]{1,0:T(8,128)(2,1)} %get-tuple-element.5.long_any), custom_call_target="tpu_custom_call" | custom-call | tf_op jit(solution)/shard_map/pallas_call | solution.py:537

commit v9 on v8

--- a/solution.py
+++ b/solution.py
@@ -28,6 +28,7 @@
 CUTS = (0, HEAD_DIM, 2 * HEAD_DIM, 4 * HEAD_DIM, 5 * HEAD_DIM)
 CHUNKS = KVHEADS
 STEPS = 8
+X_STEPS = 6
 DIRS = 4
 OWN = 2 * CHUNKS
 POOL = OWN + DIRS * STEPS
@@ -47,46 +48,54 @@
     return z * NX + x
 
 
+def routed(mask, x_first, spread, key):
+    packets = []
+    for place in range(NZ * NX):
+        z, x = divmod(place, NX)
+        goal_z, goal_x = divmod(place ^ mask, NX)
+        for chunk in range(CHUNKS):
+            dz, dx = (goal_z - z) % NZ, (goal_x - x) % NX
+            if dz > NZ // 2 or (dz == NZ // 2 and chunk % 2):
+                dz -= NZ
+            if dx > NX // 2 or (dx == NX // 2 and (chunk // spread) % 2):
+                dx -= NX
+            packets.append([place, dz, dx, chunk, chunk])
+    sends = []
+    for step in range(STEPS):
+        taken, moves = set(), []
+        for p in sorted(packets, key=key):
+            along_z = [2 if p[1] > 0 else 3] if p[1] else []
+            along_x = [0 if p[2] > 0 else 1] if p[2] and step < X_STEPS else []
+            for d in along_x + along_z if x_first else along_z + along_x:
+                if (p[0], d) not in taken:
+                    taken.add((p[0], d))
+                    moves.append((p, d))
+                    break
+        for p, d in moves:
+            sends.append((p[0], step * DIRS + d, p[3]))
+            p[0] = moved(p[0], d)
+            p[2 if d < 2 else 1] -= (1, -1)[d % 2]
+            p[3] = OWN + DIRS * step + d
+    if any(p[1] or p[2] for p in packets):
+        return None
+    return sends + [(p[0], DIRS * STEPS + p[4], p[3]) for p in packets]
+
+
 @functools.cache
 def route_table():
+    keys = [
+        lambda p: (-abs(p[1]) - abs(p[2]), -abs(p[1]), p[4]),
+        lambda p: (-abs(p[2]), -abs(p[1]), p[4]),
+        lambda p: (-abs(p[1]) - abs(p[2]), -abs(p[2]), p[4]),
+        lambda p: (-abs(p[1]), -abs(p[2]), p[4]),
+    ]
     table = np.zeros((NZ * NX, NZ * NX, ROUTE), np.int32)
     for mask in range(NZ * NX):
-        packets = []
-        for place in range(NZ * NX):
-            z, x = divmod(place, NX)
-            goal_z, goal_x = divmod(place ^ mask, NX)
-            for chunk in range(CHUNKS):
-                dz, dx = (goal_z - z) % NZ, (goal_x - x) % NX
-                if dz > NZ // 2 or (dz == NZ // 2 and chunk % 2):
-                    dz -= NZ
-                if dx > NX // 2 or (dx == NX // 2 and (chunk // (2 if mask // NX == NZ // 2 else 1)) % 2):
-                    dx -= NX
-                packets.append([place, dz, dx, chunk, chunk])
-        step = 0
-        while any(p[1] or p[2] for p in packets):
-            order = sorted(packets, key=lambda p: (-abs(p[1]) - abs(p[2]), -abs(p[1]), p[4]))
-            taken, moves = set(), []
-            for p in order:
-                options = []
-                if p[1]:
-                    options.append(2 if p[1] > 0 else 3)
-                if p[2]:
-                    options.append(0 if p[2] > 0 else 1)
-                for d in options:
-                    if (p[0], d) not in taken:
-                        taken.add((p[0], d))
-                        moves.append((p, d))
-                        break
-            for p, d in moves:
-                table[mask, p[0], step * DIRS + d] = p[3]
-                p[0] = moved(p[0], d)
-                p[2 if d < 2 else 1] -= (1, -1)[d % 2]
-                p[3] = OWN + DIRS * step + d
-            step += 1
-        assert step <= STEPS
-        for p in packets:
-            table[mask, p[0], DIRS * STEPS + p[4]] = p[3]
-    return np.ascontiguousarray(table.transpose(1, 0, 2)).reshape(-1)
+        tries = ((x_first, spread, key) for x_first in (0, 1) for spread in (1, 2) for key in keys)
+        found = next(r for r in (routed(mask, *t) for t in tries) if r is not None)
+        for place, slot, entry in found:
+            table[place, mask, slot] = entry
+    return table.reshape(-1)
 
 
 INVERSE = np.power(THETA, -np.arange(HALF, dtype=np.float64) * (2.0 / HEAD_DIM)).astype(np.float32)
@@ -231,7 +240,7 @@
         kv[0, g, :, :HEAD_DIM] = rotated(k_long[:, lanes(g, HEAD_DIM)], long_cos, long_sin)
         kv[0, g, :, HEAD_DIM:] = v_long[:, lanes(g, HEAD_DIM)]
     pl.semaphore_wait(barrier, 3 + DIRS)
-    for n in range(KVHEADS):
+    for n in range(2):
         for way in range(2):
             ring_copy(n, way).start()
 
@@ -305,27 +314,34 @@
             stage.at[slot, d], landing.at[slot, d], route_send.at[slot], route_recv.at[slot], routes[d]
         )
 
+    def used(step):
+        return range(0 if step < X_STEPS else 2, DIRS)
+
     def all_of(slot):
-        return copy(stage.at[slot], landing.at[slot], route_send.at[slot], route_recv.at[slot], routes[0])
+        dirs = used(slot // len(streams))
+        part = pl.ds(dirs[0], len(dirs))
+        return copy(
+            stage.at[slot, part], landing.at[slot, part], route_send.at[slot], route_recv.at[slot], routes[0]
+        )
 
     def collect(t, step):
         slot = len(streams) * step + t
         all_of(slot).wait_recv()
-        for d in range(DIRS):
+        for d in used(step):
             pools[t][OWN + DIRS * step + d] = landing[slot, d]
 
     def send(t, step, entries):
         slot = len(streams) * step + t
-        for d in range(DIRS):
+        for d in used(step):
             stage[slot, d] = pools[t][entries[d]]
             route_copy(slot, d).start()
 
     def ring(n):
         for way in range(2):
-            ring_copy(n, way).wait()
-        if n + KVHEADS < Y_SENDS:
-            for way in range(2):
-                ring_copy(n + KVHEADS, way).start()
+            if n > 0:
+                ring_copy(n - 1, way).wait()
+            if n + 2 < Y_SENDS:
+                ring_copy(n + 2, way).start()
 
     shift = [0] + [-h for h in range(1, HOPS + 1)] + [h for h in range(1, NY - HOPS)]
 
@@ -387,15 +403,15 @@
     loads[10].wait()
     for step in range(STEPS):
         for t in streams:
-            entries = [entry(t, step * DIRS + d) for d in range(DIRS)]
+            entries = {d: entry(t, step * DIRS + d) for d in used(step)}
             if step == 0:
                 mate_copy(t).wait()
             else:
                 collect(t, step - 1)
             send(t, step, entries)
             phase = 2 * step + t // HALVES
-            if t % HALVES == 0 and 0 < phase <= Y_SENDS:
-                ring(phase - 1)
+            if t % HALVES == 0 and phase <= Y_SENDS:
+                ring(phase)
             if t % HALVES == HALVES - 1:
                 work(plan[phase])
             if step > 0:

time: 49.5 us -> 49.1 us (level)
  the two profiles are of different devices: /device:TPU:16 before, /device:TPU:24 now
where the time goes in v9:
time: 49.1 us; the launch traced here: 48.9 us
  Pallas kernels  48.3 us (98%)
  between operations  0.64 us (1%)
    pallas_call x1, Pallas kernels, local(): pl.pallas_call(kernel, out_shape=[jax.ShapeDtypeStruct(bins_shape, bf16),...  45.9 us
    pallas_call x1, Pallas kernels, local(): pl.pallas_call(finish, out_shape=[jax.ShapeDtypeStruct(q_short.shape, bf1...  2.34 us

profile of v9, /device:TPU:24, one launch (start us, length us, event | category | flops | bytes accessed | tf_op | source)
XLA Modules:
  0.0 48.9 jit_solution(1233040823925354724)
XLA Ops:
  0.6 45.9 %shard_map.122 = (bf16[2,4,32,640]{3,2,1,0:T(8,128)(2,1)}, bf16[128,2048]{1,0:T(8,128)(2,1)}) custom-call(s32[65536]{0:T(1024)} %constant.4.clone.table_any, f32[1,128]{1,0:T(1,128)} %constant.5.clone.inverse_any, s32[1,3,2,64]{3,2,1,0:T(2,128)} %bitcast.2, s32[1,2,64]{2,1,0:T(2,128)} %bitcast.3, s32[1,3]{1,0:T(1,128)} %long_lengths_any.1, ...), custom_call_target="tpu_custom_call" | custom-call | tf_op jit(solution)/shard_map/pallas_call | solution.py:518
  46.6 2.3 %shard_map.123 = (bf16[128,2048]{1,0:T(8,128)(2,1)}, bf16[128,2048]{1,0:T(8,128)(2,1)}) custom-call(bf16[2,4,32,640]{3,2,1,0:T(8,128)(2,1)} %get-tuple-element.4.bins_any, bf16[128,2048]{1,0:T(8,128)(2,1)} %get-tuple-element.5.long_any), custom_call_target="tpu_custom_call" | custom-call | tf_op jit(solution)/shard_map/pallas_call | solution.py:553

commit v10 on v9

--- a/solution.py
+++ b/solution.py
@@ -391,9 +391,9 @@
     third = [3, HOPS + 3]
     far = [HOPS]
 
-    nearer, rest = [near, middle], third + far
-    plan = [[(prepare, 0)], [(prepare, 1)], [(prepare, 2)], [(prepare, 3)]]
-    plan += [[(attend, [g], blocks)] for blocks in nearer for g in range(KVHEADS)]
+    nearer, rest = near + middle, third + far
+    plan = [[(prepare, g) for g in range(KVHEADS)]] + [[] for _ in range(7)]
+    plan += [[(attend, [g], nearer)] for g in range(KVHEADS)]
     plan += [[], [(attend, [0], rest)], [(attend, [2], rest)], [(attend, [1], rest)]]
 
     def work(tasks):

time: 49.1 us -> 48.9 us (level)
  no operation moved by 1% of the time
where the time goes in v10:
time: 48.9 us; the launch traced here: 48.7 us
  Pallas kernels  48.1 us (98%)
  between operations  0.64 us (1%)
    pallas_call x1, Pallas kernels, local(): pl.pallas_call(kernel, out_shape=[jax.ShapeDtypeStruct(bins_shape, bf16),...  45.7 us
    pallas_call x1, Pallas kernels, local(): pl.pallas_call(finish, out_shape=[jax.ShapeDtypeStruct(q_short.shape, bf1...  2.34 us

profile of v10, /device:TPU:24, one launch (start us, length us, event | category | flops | bytes accessed | tf_op | source)
XLA Modules:
  0.0 48.7 jit_solution(2874454180689883629)
XLA Ops:
  0.6 45.7 %shard_map.122 = (bf16[2,4,32,640]{3,2,1,0:T(8,128)(2,1)}, bf16[128,2048]{1,0:T(8,128)(2,1)}) custom-call(s32[65536]{0:T(1024)} %constant.4.clone.table_any, f32[1,128]{1,0:T(1,128)} %constant.5.clone.inverse_any, s32[1,3,2,64]{3,2,1,0:T(2,128)} %bitcast.2, s32[1,2,64]{2,1,0:T(2,128)} %bitcast.3, s32[1,3]{1,0:T(1,128)} %long_lengths_any.1, ...), custom_call_target="tpu_custom_call" | custom-call | tf_op jit(solution)/shard_map/pallas_call | solution.py:518
  46.4 2.3 %shard_map.123 = (bf16[128,2048]{1,0:T(8,128)(2,1)}, bf16[128,2048]{1,0:T(8,128)(2,1)}) custom-call(bf16[2,4,32,640]{3,2,1,0:T(8,128)(2,1)} %get-tuple-element.4.bins_any, bf16[128,2048]{1,0:T(8,128)(2,1)} %get-tuple-element.5.long_any), custom_call_target="tpu_custom_call" | custom-call | tf_op jit(solution)/shard_map/pallas_call | solution.py:553

commit v11 on v9

--- a/solution.py
+++ b/solution.py
@@ -192,6 +192,10 @@
     routes = [at(z, x + 1), at(z, x - 1), at(z + 1, x), at(z - 1, x)]
     rings = [(dp, (ctx + 1) % NY), (dp, (ctx + NY - 1) % NY)]
 
+    @pl.loop(1, NY)
+    def _(i):
+        kv[i] = jnp.zeros(kv.shape[1:], kv.dtype)
+
     barrier = pltpu.get_barrier_semaphore()
     for other in [mate, *routes, *rings]:
         pl.semaphore_signal(barrier, inc=1, device_id=other, device_id_type=MESH)
@@ -213,6 +217,26 @@
         return copy(
             kv.at[source, g], kv.at[target, g], y_send.at[way, n], y_recv.at[way, n], rings[way]
         )
+
+    def goes(n, way, sender):
+        hop, g = n // KVHEADS, (n + way * (KVHEADS // 2)) % KVHEADS
+        if way == 0:
+            return (sender >= hop) & (sender < NY - 1)
+        return (sender + hop) % NY < (HOPS if g >= KVHEADS // 2 else HOPS - 1)
+
+    def ring_start(n, way):
+        @pl.when(goes(n, way, ctx))
+        def _():
+            ring_copy(n, way).start()
+
+    def ring_wait(n, way):
+        @pl.when(goes(n, way, rings[1 - way][1]))
+        def _():
+            ring_copy(n, way).wait_recv()
+
+        @pl.when(goes(n, way, ctx))
+        def _():
+            ring_copy(n, way).wait_send()
 
     for load in loads[2:5]:
         load.wait()
@@ -242,7 +266,7 @@
     pl.semaphore_wait(barrier, 3 + DIRS)
     for n in range(2):
         for way in range(2):
-            ring_copy(n, way).start()
+            ring_start(n, way)
 
     pools = [*pool_refs]
     streams = range(BINS * HALVES)
@@ -339,9 +363,9 @@
     def ring(n):
         for way in range(2):
             if n > 0:
-                ring_copy(n - 1, way).wait()
+                ring_wait(n - 1, way)
             if n + 2 < Y_SENDS:
-                ring_copy(n + 2, way).start()
+                ring_start(n + 2, way)
 
     shift = [0] + [-h for h in range(1, HOPS + 1)] + [h for h in range(1, NY - HOPS)]
 

time: 49.1 us -> 49.1 us (level)
  the two profiles are of different devices: /device:TPU:24 before, /device:TPU:16 now
where the time goes in v11:
time: 49.1 us; the launch traced here: 48.9 us
  Pallas kernels  48.3 us (98%)
  between operations  0.64 us (1%)
    pallas_call x1, Pallas kernels, local(): pl.pallas_call(kernel, out_shape=[jax.ShapeDtypeStruct(bins_shape, bf16),...  45.9 us
    pallas_call x1, Pallas kernels, local(): pl.pallas_call(finish, out_shape=[jax.ShapeDtypeStruct(q_short.shape, bf1...  2.34 us

profile of v11, /device:TPU:16, one launch (start us, length us, event | category | flops | bytes accessed | tf_op | source)
XLA Modules:
  0.0 48.9 jit_solution(919687013844233879)
XLA Ops:
  0.6 45.9 %shard_map.122 = (bf16[2,4,32,640]{3,2,1,0:T(8,128)(2,1)}, bf16[128,2048]{1,0:T(8,128)(2,1)}) custom-call(s32[65536]{0:T(1024)} %constant.4.clone.table_any, f32[1,128]{1,0:T(1,128)} %constant.5.clone.inverse_any, s32[1,3,2,64]{3,2,1,0:T(2,128)} %bitcast.2, s32[1,2,64]{2,1,0:T(2,128)} %bitcast.3, s32[1,3]{1,0:T(1,128)} %long_lengths_any.1, ...), custom_call_target="tpu_custom_call" | custom-call | tf_op jit(solution)/shard_map/pallas_call | solution.py:542
  46.5 2.3 %shard_map.123 = (bf16[128,2048]{1,0:T(8,128)(2,1)}, bf16[128,2048]{1,0:T(8,128)(2,1)}) custom-call(bf16[2,4,32,640]{3,2,1,0:T(8,128)(2,1)} %get-tuple-element.4.bins_any, bf16[128,2048]{1,0:T(8,128)(2,1)} %get-tuple-element.5.long_any), custom_call_target="tpu_custom_call" | custom-call | tf_op jit(solution)/shard_map/pallas_call | solution.py:577
